TPU v7x, 32 devices: a whole 2x2x4 slice. The times are simulated.
32 devices in a mesh: dp: 4 (over z), row: 4 (over x, core), col: 2 (over y).
Axes of the slice: x: 2, y: 2, z: 4, core: 2. Of those that a mesh axis runs over, the one named last changes fastest.
Arguments:
- layer_input: bfloat16 [16384, 768], P(('dp', 'row')), may hold values from -6 to 6
- norm_gain: float32 [768], replicated, may hold values from 0.5 to 1.5
- gate_weight: bfloat16 [768, 1536], P('row', 'col'), may hold values from -0.21875 to 0.21875
- value_weight: bfloat16 [768, 1536], P('row', 'col'), may hold values from -0.21875 to 0.21875
- state_weight: bfloat16 [768, 256], P('row'), may hold values from -0.21875 to 0.21875
- step_weight: bfloat16 [768, 24], P('row', 'col'), may hold values from -0.21875 to 0.21875
- value_kernel: float32 [4, 1536], P(None, 'col'), may hold values from -3 to 3
- value_bias: float32 [1536], P('col'), may hold values from -1.5 to 1.5
- state_kernel: float32 [4, 256], replicated, may hold values from -3 to 3
- state_bias: float32 [256], replicated, may hold values from -1.5 to 1.5
- step_bias: float32 [24], P('col'), may hold values from -5 to -2.5
- decay_log: float32 [24], P('col'), may hold values from -7 to 0.5
- skip_gain: float32 [24], P('col'), may hold values from 0.5 to 1.5
- gate_gain: float32 [1536], P('col'), may hold values from 0.5 to 1.5
- out_weight: bfloat16 [768, 1536], P('row', 'col'), may hold values from -0.15625 to 0.15625
- out_grad: bfloat16 [16384, 768], P(('dp', 'row')), may hold values from -6 to 6
Outputs:
- mixed_out: bfloat16 [16384, 768], P(('dp', 'row'))
- input_grad: float32 [16384, 768], P(('dp', 'row'))
- norm_gain_grad: float32 [768], replicated
- gate_weight_grad: float32 [768, 1536], P('row', 'col')
- value_weight_grad: float32 [768, 1536], P('row', 'col')
- state_weight_grad: float32 [768, 256], P('row')
- step_weight_grad: float32 [768, 24], P('row', 'col')
- value_kernel_grad: float32 [4, 1536], P(None, 'col')
- value_bias_grad: float32 [1536], P('col')
- state_kernel_grad: float32 [4, 256], replicated
- state_bias_grad: float32 [256], replicated
- step_bias_grad: float32 [24], P('col')
- decay_log_grad: float32 [24], P('col')
- skip_gain_grad: float32 [24], P('col')
- gate_gain_grad: float32 [1536], P('col')
- out_weight_grad: float32 [768, 1536], P('row', 'col')
All inputs are finite; a program needn't handle non-finite values.
Results may differ from a plain program's by a relative error of at most 0.00155.
The roundings to bfloat16 on the way count: a program that leaves them out, or rounds other values in their place, can miss the bound.
Values may be sent and summed in bfloat16 or wider, within the bound.
A program may use at most 192 MiB of HBM per device.

v0:
```python
import jax
import jax.numpy as jnp
from jax import lax
from jax.sharding import PartitionSpec as P

D = 768
HEADDIM = 64
STATE = 128
CONV = 4
SPAN = 256
INNER = 1536


EPSILON = 1e-05
HIGHEST = lax.Precision.HIGHEST


def from_behind(x, axis, by):
    peers = lax.axis_size(axis)
    pairs = [(i, i + by) for i in range(peers) if 0 <= i + by < peers]
    return lax.ppermute(x, axis, pairs)


def entering(value, axis, join, neutral, backward):
    count, mine = (lax.axis_size(axis), lax.axis_index(axis))
    pieces = jax.tree.map(lambda part: lax.all_gather(part, axis), value)
    if backward:
        pieces = jax.tree.map(lambda part: part[::-1], pieces)
        mine = count - 1 - mine
    total = jax.tree.map(
        lambda part, zero: jnp.full_like(part, 0) + jnp.asarray(zero, part.dtype), value, neutral
    )

    def turn(position, total):
        longer = join(total, jax.tree.map(lambda part: part[position], pieces))
        return jax.tree.map(lambda new, old: jnp.where(position < mine, new, old), longer, total)

    return lax.fori_loop(0, count - 1, turn, total)


def rms_scale(values):
    return lax.rsqrt(jnp.mean(values * values, axis=-1, keepdims=True) + EPSILON)


def conv_silu(before, kernel, kernel_bias, margin_rows):
    extended = jnp.concatenate([margin_rows, before], axis=0)
    amount = before.shape[0]
    tap_count = kernel.shape[0]
    summed = kernel_bias[None, :] + sum(
        (
            kernel[tap_index][None, :] * extended[tap_index : tap_index + amount]
            for tap_index in range(tap_count)
        )
    )
    return jax.nn.silu(summed)


def span_step(carried_in, block_data):
    carry_state, offset = carried_in
    x_heads, step_size, log_decay, b_input, c_output = block_data
    length = x_heads.shape[0]
    cumulative = jnp.cumsum(log_decay, axis=0)
    by_head = cumulative.T
    differences = by_head[:, :, None] - by_head[:, None, :]
    row_ids = lax.broadcasted_iota(jnp.int32, (length, length), 0)
    col_ids = lax.broadcasted_iota(jnp.int32, (length, length), 1)
    causal = (row_ids >= col_ids)[None]
    decays = jnp.where(causal, jnp.exp(jnp.where(causal, differences, 0.0)), 0.0)
    inner_gram = jnp.dot(c_output, b_input.T, precision=HIGHEST)
    weights = decays * inner_gram[None]
    x_scaled = x_heads * step_size[:, :, None]
    within = jnp.einsum("hts,shp->thp", weights, x_scaled, precision=HIGHEST)
    carried = jnp.einsum("tn,hpn->thp", c_output, carry_state, precision=HIGHEST)
    y_heads = within + jnp.exp(cumulative)[:, :, None] * carried
    final_cum = cumulative[-1]
    to_end = jnp.exp(final_cum[None, :] - cumulative)
    new_state = jnp.exp(final_cum)[:, None, None] * carry_state + jnp.einsum(
        "sh,shp,sn->hpn", to_end, x_scaled, b_input, precision=HIGHEST
    )
    return ((new_state, offset + final_cum), (y_heads, offset[None, :] + cumulative))


def span_scan(x_heads, step_size, log_decay, b_input, c_output):
    amount, head_part, head_width = x_heads.shape
    blocks = amount // SPAN
    carry_state = jnp.zeros((head_part, head_width, b_input.shape[1]), jnp.float32)
    offset = jnp.zeros((head_part,), jnp.float32)
    shaped = (
        x_heads.reshape(blocks, SPAN, head_part, head_width),
        step_size.reshape(blocks, SPAN, head_part),
        log_decay.reshape(blocks, SPAN, head_part),
        b_input.reshape(blocks, SPAN, -1),
        c_output.reshape(blocks, SPAN, -1),
    )
    (end_state, total_log), (y_heads, cumulative) = lax.scan(
        span_step, (carry_state, offset), shaped
    )
    return (
        y_heads.reshape(amount, head_part, head_width),
        end_state,
        total_log,
        cumulative.reshape(amount, head_part),
    )


def local_mixer(
    value_pre,
    state_pre,
    step_pre,
    rim_rows,
    value_kernel,
    value_bias,
    state_kernel,
    state_bias,
    step_bias,
    decay_log,
    skip_gain,
):
    value_width = value_pre.shape[1]
    x_conv = conv_silu(value_pre, value_kernel, value_bias, rim_rows[:, :value_width])
    bc_conv = conv_silu(state_pre, state_kernel, state_bias, rim_rows[:, value_width:])
    b_input = bc_conv[:, :STATE]
    c_output = bc_conv[:, STATE:]
    step_size = jax.nn.softplus(step_pre + step_bias)
    log_decay = -step_size * jnp.exp(decay_log)
    amount, head_part = step_pre.shape
    x_heads = x_conv.reshape(amount, head_part, HEADDIM)
    y_heads, end_state, total_log, cumulative = span_scan(
        x_heads, step_size, log_decay, b_input, c_output
    )
    y_heads = y_heads + skip_gain[None, :, None] * x_heads
    return (y_heads, jnp.exp(total_log), end_state, cumulative, c_output)


def read_entry(cumulative, c_output, entry):
    readout = jnp.einsum("tn,hpn->thp", c_output, entry, precision=HIGHEST)
    return jnp.exp(cumulative)[:, :, None] * readout


def chain_combine(earlier, later):
    return (earlier[0] * later[0], earlier[1] * later[0][:, None, None] + later[1])


def right_product(grad_low, full_weight):
    return lax.dot_general(
        grad_low, full_weight, (((1,), (1,)), ((), ())), preferred_element_type=jnp.float32
    )


def left_product(normed, grad_low):
    return lax.dot_general(
        normed, grad_low, (((0,), (0,)), ((), ())), preferred_element_type=jnp.float32
    )


def body(
    layer_input,
    norm_gain,
    gate_weight,
    value_weight,
    state_weight,
    step_weight,
    value_kernel,
    value_bias,
    state_kernel,
    state_bias,
    step_bias,
    decay_log,
    skip_gain,
    gate_gain,
    out_weight,
    out_grad,
):
    gate_full, value_full, state_full, step_full, out_full = (
        lax.all_gather(gate_weight, "row", axis=0, tiled=True),
        lax.all_gather(value_weight, "row", axis=0, tiled=True),
        lax.all_gather(state_weight, "row", axis=0, tiled=True),
        lax.all_gather(step_weight, "row", axis=0, tiled=True),
        lax.all_gather(out_weight, "row", axis=0, tiled=True),
    )
    source = layer_input.astype(jnp.float32)
    scale_in = rms_scale(source)
    normed = (source * scale_in * norm_gain).astype(jnp.bfloat16)
    gate_pre = jnp.dot(normed, gate_full, preferred_element_type=jnp.float32)
    value_pre = jnp.dot(normed, value_full, preferred_element_type=jnp.float32)
    state_pre = jnp.dot(normed, state_full, preferred_element_type=jnp.float32)
    step_pre = jnp.dot(normed, step_full, preferred_element_type=jnp.float32)
    amount, head_part = step_pre.shape
    value_width = value_pre.shape[1]
    margin = CONV - 1
    keep_prev = jnp.where(lax.axis_index("row") == 0, 0.0, 1.0).astype(jnp.float32)
    rim_send = jnp.concatenate([value_pre[amount - margin :], state_pre[amount - margin :]], axis=1)
    rim_rows = from_behind(rim_send, "row", 1) * keep_prev
    mixer_out, mixer_back = jax.vjp(
        local_mixer,
        value_pre,
        state_pre,
        step_pre,
        rim_rows,
        value_kernel,
        value_bias,
        state_kernel,
        state_bias,
        step_bias,
        decay_log,
        skip_gain,
    )
    y_local, decay_dev, state_dev, cumulative, c_output = mixer_out
    decay_kept = decay_dev * keep_prev
    identity = (jnp.ones_like(decay_dev), jnp.zeros_like(state_dev))
    prefix = entering((decay_kept, state_dev), "row", chain_combine, identity, False)
    entry = prefix[1] * keep_prev
    carried, carried_back = jax.vjp(read_entry, cumulative, c_output, entry)
    y_flat = (y_local + carried).reshape(amount, value_width)
    gate_act = jax.nn.silu(gate_pre)
    gated = y_flat * gate_act
    gate_square = lax.psum(jnp.sum(gated * gated, axis=1), "col")
    gate_scale = lax.rsqrt(gate_square / INNER + EPSILON)[:, None]
    mixed_low = (gated * gate_scale * gate_gain).astype(jnp.bfloat16)
    partial_out = right_product(mixed_low, out_full)
    summed_out = lax.psum(partial_out, "col")
    mixed_out = (source + summed_out).astype(jnp.bfloat16)
    out_weight_part = left_product(out_grad, mixed_low)
    grad_mixed = jnp.dot(out_grad, out_full, preferred_element_type=jnp.float32)
    gate_gain_part = jnp.sum(grad_mixed * gated * gate_scale, axis=0)
    gained = grad_mixed * gate_gain
    gate_inner = lax.psum(jnp.sum(gained * gated, axis=1), "col")
    grad_gated = gate_scale * gained - gated * gate_scale**3 * (gate_inner[:, None] / INNER)
    sigmoid_gate = jax.nn.sigmoid(gate_pre)
    grad_y = (grad_gated * gate_act).reshape(amount, head_part, HEADDIM)
    grad_gate_pre = grad_gated * y_flat * sigmoid_gate * (1.0 + gate_pre * (1.0 - sigmoid_gate))
    grad_cum_read, grad_c_read, grad_entry = carried_back(grad_y)
    back_prefix = entering(
        (decay_kept, grad_entry * keep_prev), "row", chain_combine, identity, True
    )
    grad_state_out = back_prefix[1]
    grad_decay_dev = jnp.sum(grad_state_out * entry, axis=(1, 2))
    (
        grad_value_pre,
        grad_state_pre,
        grad_step_pre,
        grad_rim,
        grad_value_kernel,
        grad_value_bias,
        grad_state_kernel,
        grad_state_bias,
        grad_step_bias,
        grad_decay_log,
        grad_skip_gain,
    ) = mixer_back((grad_y, grad_decay_dev, grad_state_out, grad_cum_read, grad_c_read))
    from_next = from_behind(grad_rim * keep_prev, "row", -1)
    grad_value_pre = grad_value_pre.at[amount - margin :].add(from_next[:, :value_width])
    grad_state_pre = grad_state_pre.at[amount - margin :].add(from_next[:, value_width:])
    gate_low = grad_gate_pre.astype(jnp.bfloat16)
    value_low = grad_value_pre.astype(jnp.bfloat16)
    state_low = grad_state_pre.astype(jnp.bfloat16)
    step_low = grad_step_pre.astype(jnp.bfloat16)
    grad_normed = (
        right_product(gate_low, gate_full)
        + right_product(value_low, value_full)
        + right_product(state_low, state_full)
        + right_product(step_low, step_full)
    )
    gate_weight_part = left_product(normed, gate_low)
    value_weight_part = left_product(normed, value_low)
    state_weight_part = left_product(normed, state_low)
    step_weight_part = left_product(normed, step_low)
    grad_normed, state_weight_part, grad_state_kernel, grad_state_bias = lax.psum(
        (grad_normed, state_weight_part, grad_state_kernel, grad_state_bias), "col"
    )
    gained_in = grad_normed * norm_gain
    norm_gain_part = jnp.sum(grad_normed * source * scale_in, axis=0)
    input_inner = jnp.sum(gained_in * source, axis=1, keepdims=True)
    input_grad = (
        out_grad.astype(jnp.float32)
        + scale_in * gained_in
        - source * scale_in**3 * (input_inner / D)
    )
    row_count = lax.axis_size("row")
    row_part = D // row_count
    reduced = lax.psum(
        (
            gate_weight_part,
            value_weight_part,
            state_weight_part,
            step_weight_part,
            out_weight_part,
            norm_gain_part,
            grad_value_kernel,
            grad_value_bias,
            grad_state_kernel,
            grad_state_bias,
            grad_step_bias,
            grad_decay_log,
            grad_skip_gain,
            gate_gain_part,
        ),
        ("dp", "row"),
    )
    row_start = lax.axis_index("row") * row_part
    larger_done = tuple(
        (lax.dynamic_slice_in_dim(member, row_start, row_part, 0) for member in reduced[:5])
    )
    smaller_done = reduced[5:]
    return (
        mixed_out,
        input_grad,
        smaller_done[0],
        larger_done[0],
        larger_done[1],
        larger_done[2],
        larger_done[3],
        smaller_done[1],
        smaller_done[2],
        smaller_done[3],
        smaller_done[4],
        smaller_done[5],
        smaller_done[6],
        smaller_done[7],
        smaller_done[8],
        larger_done[4],
    )


def solution(mesh):
    in_specs = (
        P(("dp", "row"), None),
        P(),
        P("row", "col"),
        P("row", "col"),
        P("row", None),
        P("row", "col"),
        P(None, "col"),
        P("col"),
        P(),
        P(),
        P("col"),
        P("col"),
        P("col"),
        P("col"),
        P("row", "col"),
        P(("dp", "row"), None),
    )
    out_specs = (
        P(("dp", "row"), None),
        P(("dp", "row"), None),
        P(),
        P("row", "col"),
        P("row", "col"),
        P("row", None),
        P("row", "col"),
        P(None, "col"),
        P("col"),
        P(),
        P(),
        P("col"),
        P("col"),
        P("col"),
        P("col"),
        P("row", "col"),
    )
    return jax.shard_map(body, mesh=mesh, in_specs=in_specs, out_specs=out_specs, check_vma=False)
```

profile of v0, /device:TPU:0, one launch (start us, length us, event | category | flops | bytes accessed | tf_op | source)
XLA Modules:
  0.0 1040.2 jit_solution(12637279294703653806)
XLA Ops:
  8.0 8.1 all_gather.37
  65.0 234.5 %while.112 = (s32[]{:T(128)}, f32[12,64,128]{2,1,0:T(8,128)S(1)}, f32[12]{0:T(128)}, f32[4,256,12,64]{1,0,3,2:T(4,128)}, f32[4,256,12]{1,0,2:T(4,128)}, /*index=...) while((s32[]{:T(128)}, f32[12,64,128]{2,1,0:T(8,128)S(1)}, ...), condition=%wide.region_4.5_spmd.clone.clone, body=%wide.region_1.4_spmd.clone.clone.sunk | while | flops 1317378048 | bytes 50723704 | solution.py:95
  86.6 17.9 %dynamic_update_slice.253 = f32[4,256,12,64]{1,0,3,2:T(4,128)} dynamic-update-slice(f32[4,256,12,64]{1,0,3,2:T(4,128)} %get-tuple-element.2594, f32[1,256,12,64]{1,0,3,2:T(1,128)S(1)} %copy.317, s32[]{:T(128)} %get-tuple-element.2591, s32[]{:T(128)} %constant.272.clone.1..sunk.3, s32[]{:T(128)} %constant.272.clone.1..sunk.3, s32[]{:T(128)} %constant.272.clone.1..sunk.3) | dynamic-update-slice | bytes 1572868 | tf_op jit(solution)/shard_map/jvp()/while/body/jit(dynamic_update_index_in_dim)/dynamic_update_slice | solution.py:95
  145.2 17.9 %dynamic_update_slice.253 = f32[4,256,12,64]{1,0,3,2:T(4,128)} dynamic-update-slice(f32[4,256,12,64]{1,0,3,2:T(4,128)} %get-tuple-element.2594, f32[1,256,12,64]{1,0,3,2:T(1,128)S(1)} %copy.317, s32[]{:T(128)} %get-tuple-element.2591, s32[]{:T(128)} %constant.272.clone.1..sunk.3, s32[]{:T(128)} %constant.272.clone.1..sunk.3, s32[]{:T(128)} %constant.272.clone.1..sunk.3) | dynamic-update-slice | bytes 1572868 | tf_op jit(solution)/shard_map/jvp()/while/body/jit(dynamic_update_index_in_dim)/dynamic_update_slice | solution.py:95
  203.8 17.9 %dynamic_update_slice.253 = f32[4,256,12,64]{1,0,3,2:T(4,128)} dynamic-update-slice(f32[4,256,12,64]{1,0,3,2:T(4,128)} %get-tuple-element.2594, f32[1,256,12,64]{1,0,3,2:T(1,128)S(1)} %copy.317, s32[]{:T(128)} %get-tuple-element.2591, s32[]{:T(128)} %constant.272.clone.1..sunk.3, s32[]{:T(128)} %constant.272.clone.1..sunk.3, s32[]{:T(128)} %constant.272.clone.1..sunk.3) | dynamic-update-slice | bytes 1572868 | tf_op jit(solution)/shard_map/jvp()/while/body/jit(dynamic_update_index_in_dim)/dynamic_update_slice | solution.py:95
  262.5 17.9 %dynamic_update_slice.253 = f32[4,256,12,64]{1,0,3,2:T(4,128)} dynamic-update-slice(f32[4,256,12,64]{1,0,3,2:T(4,128)} %get-tuple-element.2594, f32[1,256,12,64]{1,0,3,2:T(1,128)S(1)} %copy.317, s32[]{:T(128)} %get-tuple-element.2591, s32[]{:T(128)} %constant.272.clone.1..sunk.3, s32[]{:T(128)} %constant.272.clone.1..sunk.3, s32[]{:T(128)} %constant.272.clone.1..sunk.3) | dynamic-update-slice | bytes 1572868 | tf_op jit(solution)/shard_map/jvp()/while/body/jit(dynamic_update_index_in_dim)/dynamic_update_slice | solution.py:95
  304.4 6.1 all-reduce.21
  323.8 6.8 multiply_add_fusion
  339.3 6.6 multiply_reduce_fusion.9
  350.8 7.4 all-gather.14.cloned.1.call-done
  358.2 6.7 multiply_reduce_fusion.1
  369.8 8.0 multiply_reduce_fusion.2
  413.8 220.8 %while.109 = (s32[]{:T(128)}, f32[12,64,128]{2,1,0:T(8,128)S(1)}, f32[12]{0:T(128)S(1)}, f32[4,256,12,64]{1,0,3,2:T(4,128)}, f32[4,256,12]{1,0,2:T(4,128)}, /*in...) while((s32[]{:T(128)}, f32[12,64,128]{2,1,0:T(8,128)S(1)}, ...), condition=%wide.region_27.28_spmd.clone.clone, body=%wide.region_16.27_spmd.clone.clone.sunk | while | flops 2626507776 | bytes 33586592 | solution.py:95
  439.1 17.9 %dynamic_update_slice.241 = f32[4,256,12,64]{1,0,3,2:T(4,128)} dynamic-update-slice(f32[4,256,12,64]{1,0,3,2:T(4,128)} %get-tuple-element.2727, f32[1,256,12,64]{1,0,3,2:T(1,128)S(1)} %copy.304, s32[]{:T(128)S(6)} %sub.215, s32[]{:T(128)} %constant.272.clone.1..sunk, s32[]{:T(128)} %constant.272.clone.1..sunk, s32[]{:T(128)} %constant.272.clone.1..sunk) | dynamic-update-slice | bytes 1572868 | tf_op jit(solution)/shard_map/transpose(jvp())/while/body/jit(dynamic_update_index_in_dim)/dynamic_update_slice | solution.py:95
  483.0 6.1 fusion.290
  494.2 17.9 %dynamic_update_slice.241 = f32[4,256,12,64]{1,0,3,2:T(4,128)} dynamic-update-slice(f32[4,256,12,64]{1,0,3,2:T(4,128)} %get-tuple-element.2727, f32[1,256,12,64]{1,0,3,2:T(1,128)S(1)} %copy.304, s32[]{:T(128)S(6)} %sub.215, s32[]{:T(128)} %constant.272.clone.1..sunk, s32[]{:T(128)} %constant.272.clone.1..sunk, s32[]{:T(128)} %constant.272.clone.1..sunk) | dynamic-update-slice | bytes 1572868 | tf_op jit(solution)/shard_map/transpose(jvp())/while/body/jit(dynamic_update_index_in_dim)/dynamic_update_slice | solution.py:95
  538.0 6.1 fusion.290
  549.2 17.9 %dynamic_update_slice.241 = f32[4,256,12,64]{1,0,3,2:T(4,128)} dynamic-update-slice(f32[4,256,12,64]{1,0,3,2:T(4,128)} %get-tuple-element.2727, f32[1,256,12,64]{1,0,3,2:T(1,128)S(1)} %copy.304, s32[]{:T(128)S(6)} %sub.215, s32[]{:T(128)} %constant.272.clone.1..sunk, s32[]{:T(128)} %constant.272.clone.1..sunk, s32[]{:T(128)} %constant.272.clone.1..sunk) | dynamic-update-slice | bytes 1572868 | tf_op jit(solution)/shard_map/transpose(jvp())/while/body/jit(dynamic_update_index_in_dim)/dynamic_update_slice | solution.py:95
  593.1 6.1 fusion.290
  604.3 17.9 %dynamic_update_slice.241 = f32[4,256,12,64]{1,0,3,2:T(4,128)} dynamic-update-slice(f32[4,256,12,64]{1,0,3,2:T(4,128)} %get-tuple-element.2727, f32[1,256,12,64]{1,0,3,2:T(1,128)S(1)} %copy.304, s32[]{:T(128)S(6)} %sub.215, s32[]{:T(128)} %constant.272.clone.1..sunk, s32[]{:T(128)} %constant.272.clone.1..sunk, s32[]{:T(128)} %constant.272.clone.1..sunk) | dynamic-update-slice | bytes 1572868 | tf_op jit(solution)/shard_map/transpose(jvp())/while/body/jit(dynamic_update_index_in_dim)/dynamic_update_slice | solution.py:95
  642.6 9.3 multiply_reduce_fusion.5
  695.6 162.2 %all-reduce.31.cloned.1.call-done = (f32[1024,768]{1,0:T(8,128)}, f32[1024,768]{1,0:T(8,128)}, f32[768,256]{1,0:T(8,128)}) async-done(((f32[1024,768]{1,0:T(8,128)}, f32[1024,768]{1,0:T(8,128)}, f32[768,256]{1,0:T(8,128)}), (f32[1024,768]{1,0:T(8,128)}, f32[1024,768]{1,0:T(8,128)}, f32[768,256]{1,0:T(8,128)})) %all-reduce.31.cloned.1.call-update) | async-done | bytes 7077904 | tf_op jit(solution)/shard_map/psum | solution.py:221
  867.4 65.5 %all-reduce.22 = (f32[768]{0:T(1024)}, f32[768,12]{0,1:T(8,128)S(1)}, f32[4,768]{1,0:T(4,128)}, f32[768]{0:T(1024)}, f32[4,256]{1,0:T(4,128)}, /*index=5*/f32[25...) all-reduce(f32[768]{0:T(1024)S(1)} %get-tuple-element.1858, ...), channel_id=1, replica_groups=mesh['dp'=4,'row'=4,'col'=2] {'dp','row'}, use_global_device_ids=true, to_apply=%region_31.32 | all-reduce | flops 15908 | bytes 127264 | tf_op jit(solution)/shard_map/psum | solution.py:281
  938.5 88.1 %all-reduce.29.cloned.1.call-done = (f32[768,768]{1,0:T(8,128)}, f32[768,768]{1,0:T(8,128)}, f32[768,256]{1,0:T(8,128)}, f32[768,768]{0,1:T(8,128)}) async-done(((f32[768,768]{1,0:T(8,128)}, f32[768,768]{1,0:T(8,128)}, f32[768,256]{1,0:T(8,128)}, f32[768,768]{0,1:T(8,128)}), (f32[768,768]{1,0:T(8,128)}, f32[768,768]{1,0:T(8,128)}, f32[768,256]{1,0:T(8,128)}, ...) | async-done | bytes 7864336 | tf_op jit(solution)/shard_map/psum | solution.py:281
  (711 shorter events, 491.9 us)
Async XLA Ops:
  7.2 22.8 %all-gather.10.cloned.1.call-start = ((), (), s32[]{:S(2)}) async-start(), calls=%async_computation | async-start | bytes 1474560 | tf_op jit(solution)/shard_map/all_gather | solution.py:176
  7.9 312.3 %all-gather.16.cloned.1.call-start = ((), (), s32[]{:S(2)}) async-start(), calls=%async_computation.3 | async-start | bytes 1966080 | tf_op jit(solution)/shard_map/all_gather | solution.py:26
  27.0 21.8 %copy-start.65 = (f32[768]{0:T(1024)}, f32[768]{0:T(1024)S(1)}, u32[]{:S(2)}) copy-start(f32[768]{0:T(1024)S(1)} %get-tuple-element.1866) | copy-start | bytes 9220
  27.0 21.8 %copy-start.67 = (f32[768]{0:T(1024)}, f32[768]{0:T(1024)S(1)}, u32[]{:S(2)}) copy-start(f32[768]{0:T(1024)S(1)} %get-tuple-element.1867) | copy-start | bytes 9220
  27.0 21.8 %copy-start.69 = (f32[768]{0:T(1024)}, f32[768]{0:T(1024)S(1)}, u32[]{:S(2)}) copy-start(f32[768]{0:T(1024)S(1)} %get-tuple-element.1868) | copy-start | bytes 9220
  27.0 21.8 %copy-start.71 = (f32[768]{0:T(1024)}, f32[768]{0:T(1024)S(1)}, u32[]{:S(2)}) copy-start(f32[768]{0:T(1024)S(1)} %get-tuple-element.1869) | copy-start | bytes 9220
  34.9 6.9 collective-permute-start
  123.6 16.3 %copy-start.3 = (f32[4,256,12,64]{1,3,2,0:T(8,128)}, f32[4,256,12,64]{1,3,2,0:T(8,128)S(1)}, u32[]{:S(2)}) copy-start(f32[4,256,12,64]{1,3,2,0:T(8,128)S(1)} %get-tuple-element.2641) | copy-start | bytes 9437188 | tf_op jit(solution)/shard_map/jvp()/while
  182.3 16.2 %copy-start.3 = (f32[4,256,12,64]{1,3,2,0:T(8,128)}, f32[4,256,12,64]{1,3,2,0:T(8,128)S(1)}, u32[]{:S(2)}) copy-start(f32[4,256,12,64]{1,3,2,0:T(8,128)S(1)} %get-tuple-element.2641) | copy-start | bytes 9437188 | tf_op jit(solution)/shard_map/jvp()/while
  240.9 16.3 %copy-start.3 = (f32[4,256,12,64]{1,3,2,0:T(8,128)}, f32[4,256,12,64]{1,3,2,0:T(8,128)S(1)}, u32[]{:S(2)}) copy-start(f32[4,256,12,64]{1,3,2,0:T(8,128)S(1)} %get-tuple-element.2641) | copy-start | bytes 9437188 | tf_op jit(solution)/shard_map/jvp()/while
  299.6 17.8 %copy-start.5 = (f32[4,256,12,64]{1,3,2,0:T(8,128)}, f32[4,256,12,64]{1,3,2,0:T(8,128)S(1)}, u32[]{:S(2)}) copy-start(f32[4,256,12,64]{1,3,2,0:T(8,128)S(1)} %get-tuple-element.2811) | copy-start | bytes 9437188
  300.3 38.9 %all-gather.12.cloned.1.call-start = ((), (), s32[]{:S(2)}) async-start(), calls=%async_computation.1 | async-start | bytes 1474560 | tf_op jit(solution)/shard_map/all_gather | solution.py:175
  301.1 57.1 %all-gather.14.cloned.1.call-start = ((), (), s32[]{:S(2)}) async-start(), calls=%async_computation.2 | async-start | bytes 1474560 | tf_op jit(solution)/shard_map/all_gather | solution.py:179
  301.6 103.2 %all-gather.18.cloned.1.call-start = ((), (), s32[]{:S(2)}) async-start(), calls=%async_computation.4 | async-start | bytes 1966080 | tf_op jit(solution)/shard_map/all_gather | solution.py:26
  334.2 23.9 %copy-start.77 = (f32[768]{0:T(1024)S(1)}, f32[768]{0:T(1024)}, u32[]{:S(2)}) copy-start(f32[768]{0:T(1024)} %param.41) | copy-start | bytes 9220
  385.0 472.8 %all-reduce.31.cloned.1.call-start = ((), (), s32[]{:S(2)}) async-start(), calls=%async_computation.6 | async-start | bytes 14155776 | tf_op jit(solution)/shard_map/psum | solution.py:221
  439.1 27.0 %copy-start.21 = (f32[4,256,128]{2,1,0:T(8,128)S(1)}, f32[4,256,128]{2,1,0:T(8,128)}, u32[]{:S(2)}) copy-start(f32[4,256,128]{2,1,0:T(8,128)} %get-tuple-element.2768) | copy-start | bytes 1572868 | tf_op jit(solution)/shard_map/transpose(jvp())/while
  494.2 27.0 %copy-start.21 = (f32[4,256,128]{2,1,0:T(8,128)S(1)}, f32[4,256,128]{2,1,0:T(8,128)}, u32[]{:S(2)}) copy-start(f32[4,256,128]{2,1,0:T(8,128)} %get-tuple-element.2768) | copy-start | bytes 1572868 | tf_op jit(solution)/shard_map/transpose(jvp())/while
  549.2 27.0 %copy-start.21 = (f32[4,256,128]{2,1,0:T(8,128)S(1)}, f32[4,256,128]{2,1,0:T(8,128)}, u32[]{:S(2)}) copy-start(f32[4,256,128]{2,1,0:T(8,128)} %get-tuple-element.2768) | copy-start | bytes 1572868 | tf_op jit(solution)/shard_map/transpose(jvp())/while
  604.2 27.0 %copy-start.21 = (f32[4,256,128]{2,1,0:T(8,128)S(1)}, f32[4,256,128]{2,1,0:T(8,128)}, u32[]{:S(2)}) copy-start(f32[4,256,128]{2,1,0:T(8,128)} %get-tuple-element.2768) | copy-start | bytes 1572868 | tf_op jit(solution)/shard_map/transpose(jvp())/while
  665.0 7.0 collective-permute-start.1
  684.9 341.7 %all-reduce.29.cloned.1.call-start = ((), (), s32[]{:S(2)}) async-start(), calls=%async_computation.5 | async-start | bytes 15728640 | tf_op jit(solution)/shard_map/psum | solution.py:281
  863.9 69.7 %copy-start.85 = (f32[1024]{0:T(1024)S(1)}, f32[1024]{0:T(1024)}, u32[]{:S(2)}) copy-start(f32[1024]{0:T(1024)} %get-tuple-element.2078) | copy-start | bytes 12292
  864.2 69.4 %copy-start.46 = (bf16[1024,768]{1,0:T(8,128)(2,1)S(1)}, bf16[1024,768]{1,0:T(8,128)(2,1)}, u32[]{:S(2)}) copy-start(bf16[1024,768]{1,0:T(8,128)(2,1)} %param.43) | copy-start | bytes 4718596
  (126 other events, 669.2 us)
Sparse Core Ops, SparseCore 0:
  9.6 20.3 all-gather.9
  300.4 19.6 all-gather.15
  321.8 17.4 all-gather.11
  340.7 17.4 all-gather.13
  385.2 19.6 all-gather.17
  685.0 172.8 all-reduce.30
  862.4 164.1 all-reduce.28
where the time goes:
time: 1050 us; the launch traced here: 1040 us
  local copies, waits for them, and re-layouts  320 us (30%)
  waiting for transfers between devices  269 us (26%)
  matrix products  193 us (18%)
  other arithmetic  135 us (13%)
  blocking collectives  99.9 us (10%)
  between operations  16.2 us (2%)
    dynamic_update_slice x60, local copies, waits for them, and re-layouts, span_scan(): lax.scan(span_step, (carry_state, offset), shaped)  186 us
    psum x1, waiting for transfers between devices, body(): summed_out = lax.psum(partial_out, 'col')  162 us
    psum x1, waiting for transfers between devices, body(): lax.psum((gate_weight_part, value_weight_part, state_weight_part, step_we...  88.1 us
    psum x1, blocking collectives, body(): lax.psum((gate_weight_part, value_weight_part, state_weight_part, step_we...  65.5 us
    dot_general x12, matrix products, span_step(): within = jnp.einsum('hts,shp->thp', weights, x_scaled, precision=HIGHEST)  60.2 us
    dynamic_update_slice x16, other arithmetic, span_scan(): lax.scan(span_step, (carry_state, offset), shaped)  39.1 us
    dot_general x12, matrix products, span_step(): jnp.einsum('sh,shp,sn->hpn', to_end, x_scaled, b_input, precision=HIGHEST)  25.6 us
    unnamed x191, local copies, waits for them, and re-layouts  24.6 us
  transfers between devices with their start and end apart: 9, of which 7 were waited for; matrix products, arithmetic and copies ran while one was open for 8% of the time, Pallas kernels for 0%

commit v1 on v0

v1 whole, which is shorter than its diff:
```python
import functools

import jax
import jax.numpy as jnp
from jax import lax
from jax.experimental import pallas as pl
from jax.experimental.pallas import tpu as pltpu
from jax.sharding import PartitionSpec as P

D = 768
HEADDIM = 64
STATE = 128
CONV = 4
SPAN = 256
INNER = 1536


EPSILON = 1e-05
HIGHEST = lax.Precision.HIGHEST


def from_behind(x, axis, by):
    peers = lax.axis_size(axis)
    pairs = [(i, i + by) for i in range(peers) if 0 <= i + by < peers]
    return lax.ppermute(x, axis, pairs)


def entering(value, axis, join, neutral, backward):
    count, mine = (lax.axis_size(axis), lax.axis_index(axis))
    pieces = jax.tree.map(lambda part: lax.all_gather(part, axis), value)
    if backward:
        pieces = jax.tree.map(lambda part: part[::-1], pieces)
        mine = count - 1 - mine
    total = jax.tree.map(
        lambda part, zero: jnp.full_like(part, 0) + jnp.asarray(zero, part.dtype), value, neutral
    )

    def turn(position, total):
        longer = join(total, jax.tree.map(lambda part: part[position], pieces))
        return jax.tree.map(lambda new, old: jnp.where(position < mine, new, old), longer, total)

    return lax.fori_loop(0, count - 1, turn, total)


def rms_scale(values):
    return lax.rsqrt(jnp.mean(values * values, axis=-1, keepdims=True) + EPSILON)


def conv_silu(before, kernel, kernel_bias, margin_rows):
    extended = jnp.concatenate([margin_rows, before], axis=0)
    amount = before.shape[0]
    tap_count = kernel.shape[0]
    summed = kernel_bias[None, :] + sum(
        (
            kernel[tap_index][None, :] * extended[tap_index : tap_index + amount]
            for tap_index in range(tap_count)
        )
    )
    return jax.nn.silu(summed)


NN = (((1,), (0,)), ((), ()))
NT = (((1,), (1,)), ((), ()))
TN = (((0,), (0,)), ((), ()))


def split(v):
    high = v.astype(jnp.bfloat16)
    return high, (v - high.astype(jnp.float32)).astype(jnp.bfloat16)


def dot3(a, b, dims):
    def product(u, v):
        return lax.dot_general(u, v, dims, preferred_element_type=jnp.float32)

    return product(a[0], b[0]) + (product(a[0], b[1]) + product(a[1], b[0]))


def ones_dot(ones, v):
    first, second = split(v)
    third = (v - first.astype(jnp.float32) - second.astype(jnp.float32)).astype(jnp.bfloat16)

    def product(u):
        return lax.dot_general(ones, u, NN, preferred_element_type=jnp.float32)

    return product(first) + (product(second) + product(third))


def spread(per_head, pair, width):
    rows = per_head.shape[0]
    lane = lax.broadcasted_iota(jnp.int32, (rows, width), 1)
    low = jnp.broadcast_to(per_head[:, 2 * pair : 2 * pair + 1], (rows, width))
    high = jnp.broadcast_to(per_head[:, 2 * pair + 1 : 2 * pair + 2], (rows, width))
    return jnp.where(lane < HEADDIM, low, high)


def spread_all(per_head, heads):
    return jnp.concatenate([spread(per_head, j, 2 * HEADDIM) for j in range(heads // 2)], axis=1)


def decay_state(state, factor, heads):
    return jnp.concatenate(
        [state[h * HEADDIM : (h + 1) * HEADDIM] * factor[:, h : h + 1] for h in range(heads)],
        axis=0,
    )


def triangle(lower):
    rows = lax.broadcasted_iota(jnp.int32, (SPAN, SPAN), 0)
    cols = lax.broadcasted_iota(jnp.int32, (SPAN, SPAN), 1)
    return rows >= cols if lower else rows <= cols


def end_state_kernel(heads, x_ref, dt_ref, ld_ref, bc_ref, cum_ref, end_ref):
    @pl.when(pl.program_id(0) == 0)
    def _():
        end_ref[...] = jnp.zeros_like(end_ref)

    ones = triangle(True).astype(jnp.bfloat16)
    cum = ones_dot(ones, ld_ref[...])
    cum_ref[...] = cum
    final = cum[SPAN - 1 : SPAN]
    weighted = x_ref[...] * spread_all(dt_ref[...] * jnp.exp(final - cum), heads)
    added = dot3(split(weighted), split(bc_ref[:, :STATE]), TN)
    end_ref[...] = decay_state(end_ref[...], jnp.exp(final), heads) + added


def forward_kernel(heads, x_ref, dt_ref, cum_ref, cumt_ref, bc_ref, entry_ref, y_ref, s_ref, state):
    @pl.when(pl.program_id(0) == 0)
    def _():
        state[...] = entry_ref[...]

    cum = cum_ref[...]
    final = cum[SPAN - 1 : SPAN]
    b_low = split(bc_ref[:, :STATE])
    c_low = split(bc_ref[:, STATE:])
    gram = dot3(c_low, b_low, NT)
    carry = state[...]
    s_ref[0] = carry
    carried = dot3(c_low, split(carry), NT)
    causal = triangle(True)
    lane = lax.broadcasted_iota(jnp.int32, (SPAN, 2 * HEADDIM), 1)
    to_end = jnp.exp(final - cum)
    grown = jnp.exp(cum)
    weighted = []
    for j in range(heads // 2):
        at = slice(2 * HEADDIM * j, 2 * HEADDIM * (j + 1))
        xs = x_ref[:, at] * spread(dt_ref[...], j, 2 * HEADDIM)
        xs_low = split(xs)
        parts = []
        for h in (2 * j, 2 * j + 1):
            gap = cum[:, h : h + 1] - cumt_ref[h : h + 1, :]
            decay = jnp.exp(jnp.where(causal, gap, -1e30))
            parts.append(dot3(split(decay * gram), xs_low, NN))
        within = jnp.where(lane < HEADDIM, parts[0], parts[1])
        y_ref[:, at] = within + spread(grown, j, 2 * HEADDIM) * carried[:, at]
        weighted.append(xs * spread(to_end, j, 2 * HEADDIM))
    added = dot3(split(jnp.concatenate(weighted, axis=1)), b_low, TN)
    state[...] = decay_state(carry, jnp.exp(final), heads) + added


def entry_grad_kernel(heads, dy_ref, cum_ref, bc_ref, out_ref):
    @pl.when(pl.program_id(0) == 0)
    def _():
        out_ref[...] = jnp.zeros_like(out_ref)

    cum = cum_ref[...]
    grown = dy_ref[...] * spread_all(jnp.exp(cum), heads)
    added = dot3(split(grown), split(bc_ref[:, STATE:]), TN)
    out_ref[...] = decay_state(out_ref[...], jnp.exp(cum[SPAN - 1 : SPAN]), heads) + added


def backward_kernel(
    heads, x_ref, dt_ref, cum_ref, cumt_ref, bc_ref, dy_ref, y_ref, s_ref, later_ref,
    dx_ref, dbc_ref, ddt_ref, dld_ref, carry, dgram,
):
    @pl.when(pl.program_id(0) == 0)
    def _():
        carry[...] = later_ref[...]

    cum = cum_ref[...]
    final = cum[SPAN - 1 : SPAN]
    b_low = split(bc_ref[:, :STATE])
    c_low = split(bc_ref[:, STATE:])
    gram = dot3(b_low, c_low, NT)
    later = carry[...]
    later_low = split(later)
    state = s_ref[0]
    from_state = dot3(b_low, later_low, NT)
    anti = triangle(False)
    lane = lax.broadcasted_iota(jnp.int32, (SPAN, 2 * HEADDIM), 1)
    head_lane = lax.broadcasted_iota(jnp.int32, (SPAN, heads), 1)
    row = lax.broadcasted_iota(jnp.int32, (SPAN, heads), 0)
    one_lane = lax.broadcasted_iota(jnp.int32, (1, heads), 1)
    to_end = jnp.exp(final - cum)
    grown = jnp.exp(cum)
    end_factor = jnp.exp(final)
    ddt = jnp.zeros((SPAN, heads), jnp.float32)
    dcum = jnp.zeros((SPAN, heads), jnp.float32)
    dfinal = jnp.zeros((1, heads), jnp.float32)
    dgram[...] = jnp.zeros_like(dgram)
    weighted, lifted = [], []
    for j in range(heads // 2):
        at = slice(2 * HEADDIM * j, 2 * HEADDIM * (j + 1))
        x, dy = x_ref[:, at], dy_ref[:, at]
        dt = spread(dt_ref[...], j, 2 * HEADDIM)
        xs = x * dt
        xs_low, dy_low = split(xs), split(dy)
        parts = []
        for i in range(2):
            h = 2 * j + i
            mine = (lane < HEADDIM) if i == 0 else (lane >= HEADDIM)
            gap = cumt_ref[h : h + 1, :] - cum[:, h : h + 1]
            decay = jnp.exp(jnp.where(anti, gap, -1e30))
            parts.append(dot3(split(decay * gram), dy_low, NN))
            own = split(jnp.where(mine, xs, 0.0))
            dgram[...] += decay * dot3(own, dy_low, NT)
        ends = spread(to_end, j, 2 * HEADDIM)
        state_part = ends * from_state[:, at]
        dxs = jnp.where(lane < HEADDIM, parts[0], parts[1]) + state_part
        dx_ref[:, at] = dt * dxs
        weighted.append(xs * ends)
        lifted.append(dy * spread(grown, j, 2 * HEADDIM))
        over_dt = x * dxs
        over_cum = dy * y_ref[:, at] - xs * dxs
        over_end = xs * state_part
        for i in range(2):
            h = 2 * j + i
            mine = (lane < HEADDIM) if i == 0 else (lane >= HEADDIM)
            ddt = jnp.where(
                head_lane == h, jnp.sum(jnp.where(mine, over_dt, 0.0), axis=1, keepdims=True), ddt
            )
            dcum = jnp.where(
                head_lane == h, jnp.sum(jnp.where(mine, over_cum, 0.0), axis=1, keepdims=True), dcum
            )
            ending = jnp.sum(jnp.where(mine, over_end, 0.0), axis=0, keepdims=True)
            rows = slice(h * HEADDIM, (h + 1) * HEADDIM)
            held = jnp.sum(state[rows] * later[rows], axis=0, keepdims=True)
            total = jnp.sum(ending + end_factor[:, h : h + 1] * held, axis=1, keepdims=True)
            dfinal = jnp.where(one_lane == h, total, dfinal)
    ddt_ref[...] = ddt
    dcum = jnp.where(row == SPAN - 1, dcum + dfinal, dcum)
    dld_ref[...] = ones_dot(anti.astype(jnp.bfloat16), dcum)
    weighted_low = split(jnp.concatenate(weighted, axis=1))
    lifted_low = split(jnp.concatenate(lifted, axis=1))
    dgram_low = split(dgram[...])
    dbc_ref[:, :STATE] = dot3(dgram_low, c_low, NN) + dot3(weighted_low, later_low, NN)
    dbc_ref[:, STATE:] = dot3(dgram_low, b_low, TN) + dot3(lifted_low, split(state), NN)
    carry[...] = decay_state(later, end_factor, heads) + dot3(lifted_low, c_low, TN)


def chunk_call(kernel, heads, amount, in_kinds, out_kinds, backward=False, scratch=()):
    blocks = amount // SPAN

    def at(step):
        return blocks - 1 - step if backward else step

    width = heads * HEADDIM
    kinds = {
        "wide": ((amount, width), pl.BlockSpec((SPAN, width), lambda i: (at(i), 0))),
        "head": ((amount, heads), pl.BlockSpec((SPAN, heads), lambda i: (at(i), 0))),
        "headt": ((heads, amount), pl.BlockSpec((heads, SPAN), lambda i: (0, at(i)))),
        "bc": ((amount, 2 * STATE), pl.BlockSpec((SPAN, 2 * STATE), lambda i: (at(i), 0))),
        "state": ((width, STATE), pl.BlockSpec((width, STATE), lambda i: (0, 0))),
        "states": (
            (blocks, width, STATE),
            pl.BlockSpec((1, width, STATE), lambda i: (at(i), 0, 0)),
        ),
    }
    return pl.pallas_call(
        functools.partial(kernel, heads),
        grid=(blocks,),
        in_specs=[kinds[kind][1] for kind in in_kinds],
        out_specs=[kinds[kind][1] for kind in out_kinds],
        out_shape=[jax.ShapeDtypeStruct(kinds[kind][0], jnp.float32) for kind in out_kinds],
        scratch_shapes=[pltpu.VMEM(shape, jnp.float32) for shape in scratch],
        compiler_params=pltpu.CompilerParams(
            dimension_semantics=("arbitrary",), vmem_limit_bytes=48 * 2**20
        ),
    )


def ingredients(
    value_pre, state_pre, step_pre, rim_rows,
    value_kernel, value_bias, state_kernel, state_bias, step_bias, decay_log,
):
    value_width = value_pre.shape[1]
    x_conv = conv_silu(value_pre, value_kernel, value_bias, rim_rows[:, :value_width])
    bc_conv = conv_silu(state_pre, state_kernel, state_bias, rim_rows[:, value_width:])
    step_size = jax.nn.softplus(step_pre + step_bias)
    log_decay = -step_size * jnp.exp(decay_log)
    return x_conv, bc_conv, step_size, log_decay


def chain(decays, states, backward):
    count, mine = lax.axis_size("row"), lax.axis_index("row")
    order = range(count - 1, 0, -1) if backward else range(count - 1)
    total = jnp.zeros_like(states[0])
    for position in order:
        longer = jnp.repeat(decays[position], HEADDIM)[:, None] * total + states[position]
        keep = position > mine if backward else position < mine
        total = jnp.where(keep, longer, total)
    return total


def right_product(grad_low, full_weight):
    return lax.dot_general(grad_low, full_weight, NT, preferred_element_type=jnp.float32)


def left_product(normed, grad_low):
    return lax.dot_general(normed, grad_low, TN, preferred_element_type=jnp.float32)


def col_sum(part):
    return part + lax.ppermute(part, "col", [(0, 1), (1, 0)])


def body(
    layer_input,
    norm_gain,
    gate_weight,
    value_weight,
    state_weight,
    step_weight,
    value_kernel,
    value_bias,
    state_kernel,
    state_bias,
    step_bias,
    decay_log,
    skip_gain,
    gate_gain,
    out_weight,
    out_grad,
):
    value_width, state_width = value_weight.shape[1], state_weight.shape[1]
    head_part = step_weight.shape[1]
    scan_weights = lax.all_gather(
        jnp.concatenate([value_weight, state_weight, step_weight], axis=1), "row", axis=0, tiled=True
    )
    edge_weights = lax.all_gather(
        jnp.concatenate([gate_weight, out_weight], axis=1), "row", axis=0, tiled=True
    )
    gate_full, out_full = edge_weights[:, :value_width], edge_weights[:, value_width:]
    source = layer_input.astype(jnp.float32)
    scale_in = rms_scale(source)
    normed = (source * scale_in * norm_gain).astype(jnp.bfloat16)
    scan_pre = jnp.dot(normed, scan_weights, preferred_element_type=jnp.float32)
    wide = value_width + state_width
    value_pre, state_pre, step_pre = (
        scan_pre[:, :value_width], scan_pre[:, value_width:wide], scan_pre[:, wide:],
    )
    amount = normed.shape[0]
    margin = CONV - 1
    keep_prev = jnp.where(lax.axis_index("row") == 0, 0.0, 1.0).astype(jnp.float32)
    rim_rows = from_behind(scan_pre[amount - margin :, :wide], "row", 1) * keep_prev
    (x_conv, bc_conv, step_size, log_decay), ingredients_back = jax.vjp(
        ingredients, value_pre, state_pre, step_pre, rim_rows,
        value_kernel, value_bias, state_kernel, state_bias, step_bias, decay_log,
    )
    state_shape = (value_width, STATE)
    cumulative, end_state = chunk_call(
        end_state_kernel, head_part, amount, ("wide", "head", "head", "bc"), ("head", "state")
    )(x_conv, step_size, log_decay, bc_conv)
    decay_dev = jnp.exp(jnp.sum(log_decay, axis=0))
    decays = lax.all_gather(decay_dev, "row")
    end_states = lax.all_gather(end_state, "row")
    gate_pre = jnp.dot(normed, gate_full, preferred_element_type=jnp.float32)
    cumulative_t = cumulative.T
    entry = chain(decays, end_states, False)
    y_scan, states = chunk_call(
        forward_kernel, head_part, amount,
        ("wide", "head", "head", "headt", "bc", "state"), ("wide", "states"),
        scratch=(state_shape,),
    )(x_conv, step_size, cumulative, cumulative_t, bc_conv, entry)
    skip = jnp.repeat(skip_gain, HEADDIM)
    y_flat = y_scan + skip * x_conv
    grad_mixed = jnp.dot(out_grad, out_full, preferred_element_type=jnp.float32)
    sigmoid_gate = jax.nn.sigmoid(gate_pre)
    gate_act = gate_pre * sigmoid_gate
    gated = y_flat * gate_act
    gained = grad_mixed * gate_gain
    sums = col_sum(
        jnp.stack([jnp.sum(gated * gated, axis=1), jnp.sum(gained * gated, axis=1)])
    )
    gate_scale = lax.rsqrt(sums[0] / INNER + EPSILON)[:, None]
    gate_inner = sums[1][:, None] / INNER
    grad_gated = gate_scale * gained - gated * gate_scale**3 * gate_inner
    grad_y = grad_gated * gate_act
    (grad_entry,) = chunk_call(
        entry_grad_kernel, head_part, amount, ("wide", "head", "bc"), ("state",), backward=True
    )(grad_y, cumulative, bc_conv)
    grad_entries = lax.all_gather(grad_entry, "row")
    mixed_low = (gated * gate_scale * gate_gain).astype(jnp.bfloat16)
    partial_out = right_product(mixed_low, out_full)
    summed_out = col_sum(partial_out)
    mixed_out = (source + summed_out).astype(jnp.bfloat16)
    grad_gate_pre = grad_gated * y_flat * sigmoid_gate * (1.0 + gate_pre * (1.0 - sigmoid_gate))
    gate_low = grad_gate_pre.astype(jnp.bfloat16)
    early_part = jnp.concatenate(
        [left_product(out_grad, mixed_low), left_product(normed, gate_low)], axis=1
    )
    early = lax.psum(
        lax.psum_scatter(early_part, "row", scatter_dimension=0, tiled=True), "dp"
    )
    gate_gain_part = jnp.sum(grad_mixed * gated * gate_scale, axis=0)
    skip_part = jnp.sum((x_conv * grad_y).reshape(amount, head_part, HEADDIM), axis=(0, 2))
    later_grad = chain(decays, grad_entries, True)
    grad_x, grad_bc, grad_step_size, grad_log_decay = chunk_call(
        backward_kernel, head_part, amount,
        ("wide", "head", "head", "headt", "bc", "wide", "wide", "states", "state"),
        ("wide", "bc", "head", "head"),
        backward=True, scratch=(state_shape, (SPAN, SPAN)),
    )(x_conv, step_size, cumulative, cumulative_t, bc_conv, grad_y, y_scan, states, later_grad)
    (
        grad_value_pre, grad_state_pre, grad_step_pre, grad_rim,
        grad_value_kernel, grad_value_bias, grad_state_kernel, grad_state_bias,
        grad_step_bias, grad_decay_log,
    ) = ingredients_back((grad_x + skip * grad_y, grad_bc, grad_step_size, grad_log_decay))
    from_next = from_behind(grad_rim * keep_prev, "row", -1)
    grad_scan_pre = jnp.concatenate([grad_value_pre, grad_state_pre, grad_step_pre], axis=1)
    from_next = jnp.pad(from_next, ((amount - margin, 0), (0, head_part)))
    scan_low = (grad_scan_pre + from_next).astype(jnp.bfloat16)
    grad_normed_part = right_product(gate_low, gate_full) + right_product(scan_low, scan_weights)
    grad_normed = col_sum(grad_normed_part)
    late = lax.psum_scatter(
        left_product(normed, scan_low), "row", scatter_dimension=0, tiled=True
    )
    late_state = lax.psum(late[:, value_width:wide], ("dp", "col"))
    late = lax.psum(jnp.concatenate([late[:, :value_width], late[:, wide:]], axis=1), "dp")
    gained_in = grad_normed * norm_gain
    input_inner = jnp.sum(gained_in * source, axis=1, keepdims=True)
    input_grad = (
        out_grad.astype(jnp.float32)
        + scale_in * gained_in
        - source * scale_in**3 * (input_inner / D)
    )
    norm_gain_part = jnp.sum(grad_normed_part * source * scale_in, axis=0)
    shared = (norm_gain_part, grad_state_kernel, grad_state_bias)
    own = (
        grad_value_kernel, grad_value_bias, grad_step_bias, grad_decay_log, skip_part,
        gate_gain_part,
    )
    own_flat = jnp.concatenate([part.reshape(-1) for part in own])
    col = lax.axis_index("col")
    own_slots = [jnp.where(col == i, own_flat, 0.0) for i in range(lax.axis_size("col"))]
    flat = lax.psum(
        jnp.concatenate([part.reshape(-1) for part in shared] + own_slots), ("dp", "row", "col")
    )

    def take(flat, parts):
        out, start = [], 0
        for part in parts:
            out.append(flat[start : start + part.size].reshape(part.shape))
            start += part.size
        return out

    shared_size = sum(part.size for part in shared)
    norm_gain_grad, grad_state_kernel, grad_state_bias = take(flat[:shared_size], shared)
    (
        grad_value_kernel, grad_value_bias, grad_step_bias, grad_decay_log, grad_skip_gain,
        gate_gain_grad,
    ) = take(
        lax.dynamic_slice_in_dim(flat, shared_size + col * own_flat.size, own_flat.size), own
    )
    return (
        mixed_out,
        input_grad,
        norm_gain_grad,
        early[:, value_width:],
        late[:, :value_width],
        late_state,
        late[:, value_width:],
        grad_value_kernel,
        grad_value_bias,
        grad_state_kernel,
        grad_state_bias,
        grad_step_bias,
        grad_decay_log,
        grad_skip_gain,
        gate_gain_grad,
        early[:, :value_width],
    )


def solution(mesh):
    in_specs = (
        P(("dp", "row"), None),
        P(),
        P("row", "col"),
        P("row", "col"),
        P("row", None),
        P("row", "col"),
        P(None, "col"),
        P("col"),
        P(),
        P(),
        P("col"),
        P("col"),
        P("col"),
        P("col"),
        P("row", "col"),
        P(("dp", "row"), None),
    )
    out_specs = (
        P(("dp", "row"), None),
        P(("dp", "row"), None),
        P(),
        P("row", "col"),
        P("row", "col"),
        P("row", None),
        P("row", "col"),
        P(None, "col"),
        P("col"),
        P(),
        P(),
        P("col"),
        P("col"),
        P("col"),
        P("col"),
        P("row", "col"),
    )
    return jax.shard_map(body, mesh=mesh, in_specs=in_specs, out_specs=out_specs, check_vma=False)
```

time: 1050 us -> 477 us (0.45)
  local copies, waits for them, and re-layouts: 320 us -> 38.9 us
  matrix products: 193 us -> 34 us
  other arithmetic: 135 us -> 42.9 us
  waiting for transfers between devices: 269 us -> 182 us
  Pallas kernels: 0 us -> 46.2 us
    psum x2, waiting for transfers between devices: 250 us -> 62.2 us  [the longest x1 62.2 us: body(): late_state = lax.psum(late[:, value_width:wide], ('dp', 'col'))]
    dynamic_update_slice x60 -> x0, local copies, waits for them, and re-layouts: 186 us -> none  [span_scan(): lax.scan(span_step, (carry_state, offset), shaped)]
    dot_general x64 -> x7, matrix products: 180 us -> 23.1 us  [the longest x3 10.3 us: right_product(): lax.dot_general(grad_low, full_weight, NT, preferred_element_type=jnp.flo...]
    pallas_call x0 -> x4, Pallas kernels: none -> 46.2 us  [the longest x1 22.1 us: body(): chunk_call(backward_kernel, head_part, amount, ('wide', 'head', 'head', '...]
    unnamed x7 -> x9, waiting for transfers between devices: 1.95 us -> 47.7 us
    dynamic_update_slice x16 -> x0, other arithmetic: 39.1 us -> none  [span_scan(): lax.scan(span_step, (carry_state, offset), shaped)]
    all_gather x5 -> x4, waiting for transfers between devices: 17.1 us -> 54.4 us  [the longest x1 21.1 us: body(): lax.all_gather(jnp.concatenate([value_weight, state_weight, step_weight],...]
    another operation x48 -> x0, local copies, waits for them, and re-layouts: 25.1 us -> none
  transfers between devices with their start and end apart: 9 -> 13, of which waited for: 7 -> 7; matrix products, arithmetic and copies ran while one was open for 8% -> 16% of each run, Pallas kernels for 0% -> 1%
where the time goes in v1:
time: 477 us; the launch traced here: 470 us
  waiting for transfers between devices  182 us (38%)
  blocking collectives  103 us (22%)
  Pallas kernels  46.2 us (10%)
  other arithmetic  42.9 us (9%)
  local copies, waits for them, and re-layouts  38.9 us (8%)
  matrix products  34 us (7%)
  between operations  16 us (3%)
  starting transfers between devices  7.98 us (2%)
    psum x1, blocking collectives, body(): lax.psum(jnp.concatenate([part.reshape(-1) for part in shared] + own_slot...  96.2 us
    psum x1, waiting for transfers between devices, body(): late_state = lax.psum(late[:, value_width:wide], ('dp', 'col'))  62.2 us
    unnamed x9, waiting for transfers between devices  47.7 us
    unnamed x113, local copies, waits for them, and re-layouts  25 us
    pallas_call x1, Pallas kernels, body(): chunk_call(backward_kernel, head_part, amount, ('wide', 'head', 'head', '...  22.1 us
    all_gather x1, waiting for transfers between devices, body(): lax.all_gather(jnp.concatenate([value_weight, state_weight, step_weight],...  21.1 us
    all_gather x1, waiting for transfers between devices, body(): grad_entries = lax.all_gather(grad_entry, 'row')  19.4 us
    reduce_scatter x1, waiting for transfers between devices, body(): lax.psum_scatter(left_product(normed, scan_low), 'row', scatter_dimension...  15.3 us
  transfers between devices with their start and end apart: 13, of which 7 were waited for; matrix products, arithmetic and copies ran while one was open for 16% of the time, Pallas kernels for 1%

profile of v1, /device:TPU:0, one launch (start us, length us, event | category | flops | bytes accessed | tf_op | source)
XLA Modules:
  0.0 470.2 jit_solution(1508827784848634440)
XLA Ops:
  12.6 21.1 %all-gather.8.cloned.1.call-done = bf16[768,1036]{1,0:T(8,128)(2,1)} async-done(((bf16[192,1036]{1,0:T(8,128)(2,1)}), bf16[768,1036]{1,0:T(8,128)(2,1)}) %all-gather.8.cloned.1.call-update) | async-done | bytes 1591312 | tf_op jit(solution)/shard_map/all_gather | solution.py:338
  33.7 3.8 fusion.52
  46.0 6.3 %shard_map.279 = (f32[1024,12]{1,0:T(8,128)S(1)}, f32[768,128]{1,0:T(8,128)}) custom-call(f32[1024,768]{1,0:T(8,128)S(1)} %get-tuple-element.112.x_ref, f32[1024,12]{1,0:T(8,128)S(1)} %get-tuple-element.109.dt_ref, f32[1024,12]{1,0:T(8,128)S(1)} %get-tuple-element.108.ld_ref, f32[1024,256]{1,0:T(8,128)S(1)} %get-tuple-element.110.bc_ref), custom_call_target="tpu_custom_call" | custom-call | tf_op jit(solution)/shard_map/pallas_call | solution.py:362
  54.7 6.4 %all-reduce.19 = f32[48]{0:T(128)S(1)} all-reduce(f32[48]{0:T(128)S(1)} %exponential_dynamic-update-slice_fusion), channel_id=2, replica_groups=mesh['dp'=4,'row'=4,'col'=2] {'row'}, use_global_device_ids=true, to_apply=%add.19 | all-reduce | flops 48 | bytes 384
  62.8 5.1 %fusion.31 = f32[1024,768]{1,0:T(8,128)} fusion(bf16[768,1536]{1,0:T(8,128)(2,1)} %all-gather.10.cloned.1.call-done, bf16[1024,768]{1,0:T(8,128)(2,1)} %param.16, f32[768]{0:T(1024)S(1)} %copy-done.41, f32[1024]{0:T(1024)S(1)} %get-tuple-element.140), kind=kOutput, calls=%fused_computation.81 | convolution fusion | flops 1211105280 | bytes 5905408 | tf_op jit(solution)/shard_map/dot_general | solution.py:368
  67.9 13.9 %all-gather.12.cloned.1.call-done = f32[3072,128]{1,0:T(8,128)} async-done(((f32[768,128]{1,0:T(8,128)}), f32[3072,128]{1,0:T(8,128)}) %all-gather.12.cloned.1.call-update) | async-done | bytes 1572880 | tf_op jit(solution)/shard_map/all_gather | solution.py:367
  83.5 12.6 %shard_map.280 = (f32[1024,768]{1,0:T(8,128)}, f32[4,768,128]{2,1,0:T(8,128)S(1)}) custom-call(f32[1024,768]{1,0:T(8,128)} %copy-done, f32[1024,12]{1,0:T(8,128)S(1)} %copy-done.8, f32[1024,12]{1,0:T(8,128)S(1)} %copy-done.11, f32[12,1024]{1,0:T(8,128)S(1)} %bitcast.42, f32[1024,256]{1,0:T(8,128)S(1)} %copy-done.4, f32[768,128]{1,0:T(8,128)S(1)} %fusion.39.entry_ref), custom_call_target="tpu_custom_call" | custom-call | tf_op jit(solution)/shard_map/pallas_call | solution.py:371
  96.1 5.7 %multiply_reduce_fusion.6 = (f32[1024]{0:T(1024)S(1)}, f32[1024]{0:T(1024)S(1)}, f32[1024,768]{1,0:T(8,128)S(1)}, f32[768,1024]{0,1:T(8,128)S(1)}) fusion(f32[768]{0:T(1024)S(1)} %copy-done.40, f32[1024,768]{1,0:T(8,128)} %fusion.31, f32[1024,768]{1,0:T(8,128)} %get-tuple-element.26.y_ref, f32[1024,768]{1,0:T(8,128)S(1)} %copy-done.18, f32[768]{0:T(1024)S(1)} %mul.496, ...), kind=kOutput, calls=%fused_computation.41 | convolution fusion | flops 1220540416 | bytes 18495488 | tf_op jit(solution)/shard_map/dot_general | solution.py:378
  105.7 4.5 multiply_reduce_fusion
  110.2 5.2 %shard_map.281 = f32[768,128]{1,0:T(8,128)} custom-call(f32[1024,768]{1,0:T(8,128)S(1)} %get-tuple-element.101.dy_ref, f32[1024,12]{1,0:T(8,128)S(1)} %copy-done.12, f32[1024,256]{1,0:T(8,128)S(1)} %copy-done.5), custom_call_target="tpu_custom_call" | custom-call | tf_op jit(solution)/shard_map/pallas_call | solution.py:390
  115.9 19.4 %all-gather.14.cloned.1.call-done = f32[3072,128]{1,0:T(8,128)} async-done(((f32[768,128]{1,0:T(8,128)}), f32[3072,128]{1,0:T(8,128)}) %all-gather.14.cloned.1.call-update) | async-done | bytes 1572880 | tf_op jit(solution)/shard_map/all_gather | solution.py:393
  141.6 22.1 %shard_map.282 = (f32[1024,768]{1,0:T(8,128)}, f32[1024,256]{1,0:T(8,128)S(1)}, f32[1024,12]{1,0:T(8,128)S(1)}, f32[1024,12]{1,0:T(8,128)S(1)}) custom-call(f32[1024,768]{1,0:T(8,128)} %copy-done, f32[1024,12]{1,0:T(8,128)S(1)} %copy-done.9, f32[1024,12]{1,0:T(8,128)S(1)} %copy-done.13, f32[12,1024]{1,0:T(8,128)S(1)} %bitcast.43, f32[1024,256]{1,0:T(8,128)S(1)} %copy-done.6, ...), custom_call_target="tpu_custom_call" | custom-call | tf_op jit(solution)/shard_map/pallas_call | solution.py:409
  163.7 5.1 %multiply_reduce_fusion.3 = (f32[768]{0:T(1024)S(1)}, f32[768]{0:T(1024)S(1)}, f32[768]{0:T(1024)S(1)}, f32[768]{0:T(1024)S(1)}, f32[768]{0:T(1024)S(1)}, /*index=5*/f32[1024,768]{1,0:T(8,128)S(1)}) fusion(f32[1024,768]{1,0:T(8,128)S(1)} %copy-done.17, f32[3,768]{1,0:T(4,128)S(1)} %slice.217, f32[1024,1036]{1,0:T(8,128)} %copy-done.20, ...), kind=kLoop, calls=%fused_computation.34 | loop fusion | flops 18084096 | bytes 18902016 | tf_op jit(solution)/shard_map/transpose(jvp())/reduce_sum | solution.py:55
  179.7 4.2 fusion.45
  184.0 3.2 fusion.49
  191.3 6.3 %copy.64 = f32[768,1536]{1,0:T(8,128)} copy(f32[768,1536]{0,1:T(8,128)} %pad_maximum_fusion) | data formatting | bytes 9437184
  198.0 3.3 fusion.29
  201.7 3.9 convolution_add_fusion
  211.1 15.3 %reduce-scatter.5.cloned.1.call-done = f32[192,1036]{1,0:T(8,128)} async-done(((f32[768,1036]{1,0:T(8,128)}), f32[192,1036]{1,0:T(8,128)}) %reduce-scatter.5.cloned.1.call-update) | async-done | bytes 795664 | tf_op jit(solution)/shard_map/reduce_scatter | solution.py:426
  229.3 47.5 %reduce-scatter.7.cloned.1.call-done = f32[192,1536]{1,0:T(8,128)} async-done(((f32[768,1536]{1,0:T(8,128)}), f32[192,1536]{1,0:T(8,128)}) %reduce-scatter.7.cloned.1.call-update) | async-done | bytes 1179664
  279.9 4.2 fusion.13
  284.1 96.2 %psum.28 = f32[11336]{0:T(1024)S(1)} all-reduce(f32[11336]{0:T(1024)S(1)} %concatenate.33), channel_id=1, replica_groups=mesh['dp'=4,'row'=4,'col'=2] {'dp','row','col'}, use_global_device_ids=true, to_apply=%region_21.22 | all-reduce | flops 11336 | bytes 90688 | tf_op jit(solution)/shard_map/psum | solution.py:447
  383.4 7.0 %fusion.10 = (f32[1024,768]{1,0:T(8,128)}, bf16[1024,768]{1,0:T(8,128)(2,1)}) fusion(bf16[1024,768]{1,0:T(8,128)(2,1)S(1)} %copy-done.22, bf16[1024,768]{1,0:T(8,128)(2,1)S(1)} %copy-done.34, f32[1024]{0:T(1024)S(1)} %broadcast_multiply_fusion.9, f32[1024]{0:T(1024)S(1)} %get-tuple-element.139, f32[1024]{0:T(1024)S(1)} %get-tuple-element.140, ...), kind=kLoop, calls=%fused_computation.22 | loop fusion | flops 9437184 | bytes 20462592 | tf_op jit(solution)/shard_map/sub | solution.py:434
  399.3 62.2 %all-reduce.24.cloned.1.call-done = f32[192,256]{1,0:T(8,128)} async-done(((f32[192,256]{1,0:T(8,128)}), f32[192,256]{1,0:T(8,128)}) %all-reduce.24.cloned.1.call-update) | async-done | bytes 196624 | tf_op jit(solution)/shard_map/psum | solution.py:429
  (216 shorter events, 69.8 us)
Async XLA Ops:
  7.2 26.5 %copy-start.41 = (f32[768]{0:T(1024)S(1)}, f32[768]{0:T(1024)}, u32[]{:S(2)}) copy-start(f32[768]{0:T(1024)} %param.17) | copy-start | bytes 9220
  7.2 26.5 %all-gather.8.cloned.1.call-start = ((), (), s32[]{:S(2)}) async-start(), calls=%async_computation.2 | async-start | bytes 2211840 | tf_op jit(solution)/shard_map/all_gather | solution.py:338
  10.1 52.7 %all-gather.10.cloned.1.call-start = ((), (), s32[]{:S(2)}) async-start(), calls=%async_computation.3 | async-start | bytes 2949120 | tf_op jit(solution)/shard_map/all_gather | solution.py:341
  12.0 69.8 %all-gather.12.cloned.1.call-start = ((), (), s32[]{:S(2)}) async-start(), calls=%async_computation.6 | async-start | bytes 1966080 | tf_op jit(solution)/shard_map/all_gather | solution.py:367
  37.5 3.0 collective-permute-start
  46.0 16.8 %copy-start = (f32[1024,768]{1,0:T(8,128)}, f32[1024,768]{1,0:T(8,128)S(1)}, u32[]{:S(2)}) copy-start(f32[1024,768]{1,0:T(8,128)S(1)} %get-tuple-element.112.x_ref) | copy-start | bytes 9437188
  53.1 82.2 %all-gather.14.cloned.1.call-start = ((), (), s32[]{:S(2)}) async-start(), calls=%async_computation.7 | async-start | bytes 1966080 | tf_op jit(solution)/shard_map/all_gather | solution.py:393
  62.8 20.7 %copy-start.4 = (f32[1024,256]{1,0:T(8,128)S(1)}, f32[1024,256]{1,0:T(8,128)}, u32[]{:S(2)}) copy-start(f32[1024,256]{1,0:T(8,128)} %copy-done.3) | copy-start | bytes 3145732
  62.8 20.7 %copy-start.8 = (f32[1024,12]{1,0:T(8,128)S(1)}, f32[1024,12]{1,0:T(8,128)}, u32[]{:S(2)}) copy-start(f32[1024,12]{1,0:T(8,128)} %copy-done.7) | copy-start | bytes 147460
  62.8 20.7 %copy-start.11 = (f32[1024,12]{1,0:T(8,128)S(1)}, f32[1024,12]{1,0:T(8,128)}, u32[]{:S(2)}) copy-start(f32[1024,12]{1,0:T(8,128)} %copy-done.10) | copy-start | bytes 147460
  83.4 12.7 %copy-start.18 = (f32[1024,768]{1,0:T(8,128)S(1)}, f32[1024,768]{1,0:T(8,128)}, u32[]{:S(2)}) copy-start(f32[1024,768]{1,0:T(8,128)} %get-tuple-element.113) | copy-start | bytes 9437188
  83.4 12.7 %copy-start.33 = (bf16[1024,768]{1,0:T(8,128)(2,1)S(1)}, bf16[1024,768]{1,0:T(8,128)(2,1)}, u32[]{:S(2)}) copy-start(bf16[1024,768]{1,0:T(8,128)(2,1)} %param.31) | copy-start | bytes 4718596
  101.9 3.7 collective-permute-start.1
  110.2 26.7 %copy-start.1 = (f32[1024,768]{1,0:T(8,128)}, f32[1024,768]{1,0:T(8,128)S(1)}, u32[]{:S(2)}) copy-start(f32[1024,768]{1,0:T(8,128)S(1)} %get-tuple-element.101.dy_ref) | copy-start | bytes 9437188
  115.5 110.9 %reduce-scatter.5.cloned.1.call-start = ((), (), s32[]{:S(2)}) async-start(), calls=%async_computation.4 | async-start | bytes 4423680 | tf_op jit(solution)/shard_map/reduce_scatter | solution.py:426
  141.6 22.1 %copy-start.2 = (f32[1024,768]{1,0:T(8,128)S(1)}, f32[1024,768]{1,0:T(8,128)}, u32[]{:S(2)}) copy-start(f32[1024,768]{1,0:T(8,128)} %copy-done.1) | copy-start | bytes 9437188
  141.6 22.1 %copy-start.17 = (f32[1024,768]{1,0:T(8,128)S(1)}, f32[1024,768]{1,0:T(8,128)}, u32[]{:S(2)}) copy-start(f32[1024,768]{1,0:T(8,128)} %copy-done.16) | copy-start | bytes 9437188
  141.6 22.1 %copy-start.19 = (f32[1024,768]{1,0:T(8,128)S(1)}, f32[1024,768]{1,0:T(8,128)}, u32[]{:S(2)}) copy-start(f32[1024,768]{1,0:T(8,128)} %get-tuple-element.113) | copy-start | bytes 9437188
  173.8 3.5 collective-permute-start.3
  183.9 92.9 %reduce-scatter.7.cloned.1.call-start = ((), (), s32[]{:S(2)}) async-start(), calls=%async_computation.8 | async-start | bytes 5898240
  197.6 194.5 %all-reduce.26.cloned.1.call-start = ((), (), s32[]{:S(2)}) async-start(), calls=%async_computation.9 | async-start | bytes 4521984 | tf_op jit(solution)/shard_map/psum | solution.py:403
  205.6 74.3 %collective-permute-start.4 = (f32[1024,768]{1,0:T(8,128)}, f32[1024,768]{1,0:T(8,128)}, u32[]{:S(2)}, u32[]{:S(2)}) collective-permute-start(f32[1024,768]{1,0:T(8,128)} %convolution_add_fusion), channel_id=1, source_target_pairs={{0,1},{1,0},{2,3},{3,2},{4,5},{5,4},{6,7},{7,6},{8,9},{9,8},{10,11... | collective-permute-start | bytes 9437192 | tf_op jit(solution)/shard_map/ppermute | solution.py:315
  210.3 173.2 %collective-permute-start.2 = (f32[1024,768]{1,0:T(8,128)}, f32[1024,768]{1,0:T(8,128)}, u32[]{:S(2)}, u32[]{:S(2)}) collective-permute-start(f32[1024,768]{1,0:T(8,128)} %fusion.25), channel_id=1, source_target_pairs={{0,1},{1,0},{2,3},{3,2},{4,5},{5,4},{6,7},{7,6},{8,9},{9,8},{10,11... | collective-permute-start | bytes 9437192 | tf_op jit(solution)/shard_map/ppermute | solution.py:315
  279.8 181.7 %all-reduce.24.cloned.1.call-start = ((), (), s32[]{:S(2)}) async-start(), calls=%async_computation.5 | async-start | bytes 393216 | tf_op jit(solution)/shard_map/psum | solution.py:429
  (40 other events, 163.4 us)
Sparse Core Ops, SparseCore 0:
  10.2 23.4 all-gather.7
  35.8 24.0 all-gather.9
  62.1 19.7 all-gather.11
  115.6 19.6 all-gather.13
  184.0 42.3 reduce-scatter.4
  229.0 47.8 reduce-scatter.6
  279.9 93.7 all-reduce.25
  392.2 69.1 all-reduce.23

commit v2 on v1

--- a/solution.py
+++ b/solution.py
@@ -249,7 +249,9 @@
     carry[...] = decay_state(later, end_factor, heads) + dot3(lifted_low, c_low, TN)
 
 
-def chunk_call(kernel, heads, amount, in_kinds, out_kinds, backward=False, scratch=()):
+def chunk_call(
+    kernel, heads, amount, in_kinds, out_kinds, backward=False, scratch=(), flops=4096
+):
     blocks = amount // SPAN
 
     def at(step):
@@ -274,6 +276,9 @@
         out_specs=[kinds[kind][1] for kind in out_kinds],
         out_shape=[jax.ShapeDtypeStruct(kinds[kind][0], jnp.float32) for kind in out_kinds],
         scratch_shapes=[pltpu.VMEM(shape, jnp.float32) for shape in scratch],
+        cost_estimate=pl.CostEstimate(
+            flops=flops * amount * width, bytes_accessed=2**24, transcendentals=amount * width
+        ),
         compiler_params=pltpu.CompilerParams(
             dimension_semantics=("arbitrary",), vmem_limit_bytes=48 * 2**20
         ),
@@ -292,15 +297,49 @@
     return x_conv, bc_conv, step_size, log_decay
 
 
-def chain(decays, states, backward):
-    count, mine = lax.axis_size("row"), lax.axis_index("row")
-    order = range(count - 1, 0, -1) if backward else range(count - 1)
-    total = jnp.zeros_like(states[0])
-    for position in order:
-        longer = jnp.repeat(decays[position], HEADDIM)[:, None] * total + states[position]
-        keep = position > mine if backward else position < mine
-        total = jnp.where(keep, longer, total)
+def chain(decay, states, way):
+    factor = jnp.ones_like(decay)
+    total = from_behind(states, "row", way)
+    for by in range(1, lax.axis_size("row") - 1):
+        factor = factor * from_behind(decay, "row", way * by)
+        piece = from_behind(states, "row", way * (by + 1))
+        total = total + jnp.repeat(factor, HEADDIM)[:, None] * piece
     return total
+
+
+def butterfly(part, axis):
+    peers = lax.axis_size(axis)
+    by = 1
+    while by < peers:
+        part = part + lax.ppermute(part, axis, [(i, i ^ by) for i in range(peers)])
+        by *= 2
+    return part
+
+
+def halves_in(part, axis):
+    peers, me = lax.axis_size(axis), lax.axis_index(axis)
+    by = 1
+    while by < peers:
+        odd = (me // by) % 2 == 1
+        half = part.shape[0] // 2
+        first, second = part[:half], part[half:]
+        given = lax.ppermute(
+            jnp.where(odd, first, second), axis, [(i, i ^ by) for i in range(peers)]
+        )
+        part = jnp.where(odd, second, first) + given
+        by *= 2
+    return part
+
+
+def halves_out(part, axis):
+    peers, me = lax.axis_size(axis), lax.axis_index(axis)
+    by = peers // 2
+    while by >= 1:
+        odd = (me // by) % 2 == 1
+        given = lax.ppermute(part, axis, [(i, i ^ by) for i in range(peers)])
+        part = jnp.concatenate([jnp.where(odd, given, part), jnp.where(odd, part, given)], axis=0)
+        by //= 2
+    return part
 
 
 def right_product(grad_low, full_weight):
@@ -363,11 +402,9 @@
         end_state_kernel, head_part, amount, ("wide", "head", "head", "bc"), ("head", "state")
     )(x_conv, step_size, log_decay, bc_conv)
     decay_dev = jnp.exp(jnp.sum(log_decay, axis=0))
-    decays = lax.all_gather(decay_dev, "row")
-    end_states = lax.all_gather(end_state, "row")
     gate_pre = jnp.dot(normed, gate_full, preferred_element_type=jnp.float32)
     cumulative_t = cumulative.T
-    entry = chain(decays, end_states, False)
+    entry = chain(decay_dev, end_state, 1)
     y_scan, states = chunk_call(
         forward_kernel, head_part, amount,
         ("wide", "head", "head", "headt", "bc", "state"), ("wide", "states"),
@@ -390,28 +427,27 @@
     (grad_entry,) = chunk_call(
         entry_grad_kernel, head_part, amount, ("wide", "head", "bc"), ("state",), backward=True
     )(grad_y, cumulative, bc_conv)
-    grad_entries = lax.all_gather(grad_entry, "row")
     mixed_low = (gated * gate_scale * gate_gain).astype(jnp.bfloat16)
     partial_out = right_product(mixed_low, out_full)
     summed_out = col_sum(partial_out)
-    mixed_out = (source + summed_out).astype(jnp.bfloat16)
     grad_gate_pre = grad_gated * y_flat * sigmoid_gate * (1.0 + gate_pre * (1.0 - sigmoid_gate))
     gate_low = grad_gate_pre.astype(jnp.bfloat16)
     early_part = jnp.concatenate(
         [left_product(out_grad, mixed_low), left_product(normed, gate_low)], axis=1
     )
-    early = lax.psum(
-        lax.psum_scatter(early_part, "row", scatter_dimension=0, tiled=True), "dp"
-    )
     gate_gain_part = jnp.sum(grad_mixed * gated * gate_scale, axis=0)
     skip_part = jnp.sum((x_conv * grad_y).reshape(amount, head_part, HEADDIM), axis=(0, 2))
-    later_grad = chain(decays, grad_entries, True)
+    later_grad = chain(decay_dev, grad_entry, -1)
+    early_part, later_grad = lax.optimization_barrier((early_part, later_grad))
+    early = lax.psum_scatter(early_part, "row", scatter_dimension=0, tiled=True)
     grad_x, grad_bc, grad_step_size, grad_log_decay = chunk_call(
         backward_kernel, head_part, amount,
         ("wide", "head", "head", "headt", "bc", "wide", "wide", "states", "state"),
         ("wide", "bc", "head", "head"),
-        backward=True, scratch=(state_shape, (SPAN, SPAN)),
+        backward=True, scratch=(state_shape, (SPAN, SPAN)), flops=16384,
     )(x_conv, step_size, cumulative, cumulative_t, bc_conv, grad_y, y_scan, states, later_grad)
+    grad_x, summed_out = lax.optimization_barrier((grad_x, summed_out))
+    mixed_out = (source + summed_out).astype(jnp.bfloat16)
     (
         grad_value_pre, grad_state_pre, grad_step_pre, grad_rim,
         grad_value_kernel, grad_value_bias, grad_state_kernel, grad_state_bias,
@@ -421,13 +457,19 @@
     grad_scan_pre = jnp.concatenate([grad_value_pre, grad_state_pre, grad_step_pre], axis=1)
     from_next = jnp.pad(from_next, ((amount - margin, 0), (0, head_part)))
     scan_low = (grad_scan_pre + from_next).astype(jnp.bfloat16)
+    scan_low, early = lax.optimization_barrier((scan_low, early))
+    early = halves_in(early, "dp")
     grad_normed_part = right_product(gate_low, gate_full) + right_product(scan_low, scan_weights)
     grad_normed = col_sum(grad_normed_part)
     late = lax.psum_scatter(
         left_product(normed, scan_low), "row", scatter_dimension=0, tiled=True
     )
-    late_state = lax.psum(late[:, value_width:wide], ("dp", "col"))
-    late = lax.psum(jnp.concatenate([late[:, :value_width], late[:, wide:]], axis=1), "dp")
+    late = jnp.concatenate(
+        [late[:, :value_width], col_sum(late[:, value_width:wide]), late[:, wide:]], axis=1
+    )
+    late, early = lax.optimization_barrier((late, early))
+    early = halves_out(early, "dp")
+    late = halves_out(halves_in(late, "dp"), "dp")
     gained_in = grad_normed * norm_gain
     input_inner = jnp.sum(gained_in * source, axis=1, keepdims=True)
     input_grad = (
@@ -444,9 +486,9 @@
     own_flat = jnp.concatenate([part.reshape(-1) for part in own])
     col = lax.axis_index("col")
     own_slots = [jnp.where(col == i, own_flat, 0.0) for i in range(lax.axis_size("col"))]
-    flat = lax.psum(
-        jnp.concatenate([part.reshape(-1) for part in shared] + own_slots), ("dp", "row", "col")
-    )
+    flat = jnp.concatenate([part.reshape(-1) for part in shared] + own_slots)
+    for axis in ("row", "col", "dp"):
+        flat = butterfly(flat, axis)
 
     def take(flat, parts):
         out, start = [], 0
@@ -469,8 +511,8 @@
         norm_gain_grad,
         early[:, value_width:],
         late[:, :value_width],
-        late_state,
-        late[:, value_width:],
+        late[:, value_width:wide],
+        late[:, wide:],
         grad_value_kernel,
         grad_value_bias,
         grad_state_kernel,

time: 477 us -> 426 us (0.89)
  blocking collectives: 103 us -> 0 us
  starting transfers between devices: 7.98 us -> 45 us
  other arithmetic: 42.9 us -> 57.9 us
  waiting for transfers between devices: 182 us -> 192 us
  local copies, waits for them, and re-layouts: 38.9 us -> 33.5 us
    psum x1 -> x0, blocking collectives: 96.2 us -> none  [body(): lax.psum(jnp.concatenate([part.reshape(-1) for part in shared] + own_slot...]
    ppermute x3 -> x4, waiting for transfers between devices: 2.17 us -> 85.8 us  [col_sum(): return part + lax.ppermute(part, 'col', [(0, 1), (1, 0)])]
    psum x2 -> x0, waiting for transfers between devices: 62.2 us -> none  [the longest x1 62.2 us: body(): late_state = lax.psum(late[:, value_width:wide], ('dp', 'col'))]
    ppermute x0 -> x13, waiting for transfers between devices: none -> 59.6 us  [the longest x4 33.3 us: halves_out(): given = lax.ppermute(part, axis, [(i, i ^ by) for i in range(peers)])]
    unnamed x9 -> x5, waiting for transfers between devices: 47.7 us -> 0.07 us
    all_gather x2 -> x0, waiting for transfers between devices: 33.3 us -> none  [the longest x1 19.4 us: body(): grad_entries = lax.all_gather(grad_entry, 'row')]
    ppermute x2 -> x12, waiting for transfers between devices: 0.04 us -> 25.5 us  [from_behind(): return lax.ppermute(x, axis, pairs)]
    ppermute x0 -> x13, starting transfers between devices: none -> 22.1 us  [the longest x5 12.6 us: butterfly(): part = part + lax.ppermute(part, axis, [(i, i ^ by) for i in range(peers)])]
  transfers between devices with their start and end apart: 13 -> 33, of which waited for: 7 -> 20; matrix products, arithmetic and copies ran while one was open for 16% -> 19% of each run, Pallas kernels for 1% -> 10%
where the time goes in v2:
time: 426 us; the launch traced here: 420 us
  waiting for transfers between devices  192 us (45%)
  other arithmetic  57.9 us (14%)
  starting transfers between devices  45 us (11%)
  Pallas kernels  44.6 us (10%)
  local copies, waits for them, and re-layouts  33.5 us (8%)
  matrix products  31.5 us (7%)
  between operations  15 us (4%)
    ppermute x4, waiting for transfers between devices, col_sum(): return part + lax.ppermute(part, 'col', [(0, 1), (1, 0)])  85.8 us
    ppermute x4, waiting for transfers between devices, halves_out(): given = lax.ppermute(part, axis, [(i, i ^ by) for i in range(peers)])  33.3 us
    ppermute x12, waiting for transfers between devices, from_behind(): return lax.ppermute(x, axis, pairs)  25.5 us
    pallas_call x1, Pallas kernels, body(): chunk_call(backward_kernel, head_part, amount, ('wide', 'head', 'head', '...  22 us
    all_gather x1, waiting for transfers between devices, body(): lax.all_gather(jnp.concatenate([value_weight, state_weight, step_weight],...  21.1 us
    ppermute x4, waiting for transfers between devices, halves_in(): lax.ppermute(jnp.where(odd, first, second), axis, [(i, i ^ by) for i in r...  21 us
    ppermute x12, starting transfers between devices, from_behind(): return lax.ppermute(x, axis, pairs)  19.4 us
    unnamed x96, local copies, waits for them, and re-layouts  16.6 us
  transfers between devices with their start and end apart: 33, of which 20 were waited for; matrix products, arithmetic and copies ran while one was open for 19% of the time, Pallas kernels for 10%

profile of v2, /device:TPU:0, one launch (start us, length us, event | category | flops | bytes accessed | tf_op | source)
XLA Modules:
  0.0 419.5 jit_solution(4048084124827193818)
XLA Ops:
  12.6 21.1 %all-gather.3.cloned.1.call-done = bf16[768,1036]{1,0:T(8,128)(2,1)} async-done(((bf16[192,1036]{1,0:T(8,128)(2,1)}), bf16[768,1036]{1,0:T(8,128)(2,1)}) %all-gather.3.cloned.1.call-update) | async-done | bytes 1591312 | tf_op jit(solution)/shard_map/all_gather | solution.py:377
  46.0 5.5 %shard_map.279 = (f32[1024,12]{1,0:T(8,128)S(1)}, f32[768,128]{1,0:T(8,128)S(1)}) custom-call(f32[1024,768]{1,0:T(8,128)S(1)} %get-tuple-element.126.x_ref, f32[1024,12]{1,0:T(8,128)S(1)} %get-tuple-element.123.dt_ref, f32[1024,12]{1,0:T(8,128)S(1)} %get-tuple-element.122.ld_ref, f32[1024,256]{1,0:T(8,128)S(1)} %get-tuple-element.124.bc_ref), custom_call_target="tpu_custom_call" | custom-call | flops 3221225472 | bytes 16777216 | tf_op jit(solution)/shard_map/pallas_call | solution.py:401
  61.6 11.3 %collective-permute-done.4 = f32[12]{0:T(128)S(1)} collective-permute-done((f32[12]{0:T(128)S(1)}, f32[12]{0:T(128)S(1)}, u32[]{:S(2)}, u32[]{:S(2)}) %collective-permute-start.4) | collective-permute-done | bytes 80 | tf_op jit(solution)/shard_map/ppermute | solution.py:25
  76.8 12.5 %shard_map.280 = (f32[1024,768]{1,0:T(8,128)}, f32[4,768,128]{2,1,0:T(8,128)S(1)}) custom-call(f32[1024,768]{1,0:T(8,128)} %copy-done.2, f32[1024,12]{1,0:T(8,128)S(1)} %copy-done.4, f32[1024,12]{1,0:T(8,128)S(1)} %get-tuple-element.32.cum_ref, f32[12,1024]{1,0:T(8,128)S(1)} %bitcast.43, f32[1024,256]{1,0:T(8,128)S(1)} %copy-done.7, ...), custom_call_target="tpu_custom_call" | custom-call | flops 3221225472 | bytes 16777216 | tf_op jit(solution)/shard_map/pallas_call | solution.py:408
  95.8 4.9 %multiply_reduce_fusion.6 = (f32[1024]{0:T(1024)S(1)}, f32[1024]{0:T(1024)S(1)}, f32[1024,768]{1,0:T(8,128)}, f32[768,1024]{0,1:T(8,128)}) fusion(f32[768]{0:T(1024)S(1)} %copy-done.33, f32[1024,768]{1,0:T(8,128)S(1)} %fusion.31, f32[1024,768]{1,0:T(8,128)S(1)} %copy-done.25, f32[1024,768]{1,0:T(8,128)S(1)} %copy-done.14, f32[768]{0:T(1024)S(1)} %mul.475, ...), kind=kOutput, calls=%fused_computation.41 | convolution fusion | flops 1220540416 | bytes 18497536 | tf_op jit(solution)/shard_map/dot_general | solution.py:415
  108.5 7.3 %multiply_reduce_fusion = (f32[768]{0:T(1024)S(1)}, f32[1024,768]{1,0:T(8,128)S(1)}, bf16[1024,768]{1,0:T(8,128)(2,1)S(1)}, f32[768]{0:T(1024)S(1)}) fusion(f32[1024,768]{1,0:T(8,128)} %get-tuple-element.127, f32[1024,768]{1,0:T(8,128)} %copy-done.27, f32[1024]{0:T(1024)S(1)} %bitcast.51, f32[1024,768]{1,0:T(8,128)} %get-tuple-element.120, ...), kind=kLoop, calls=%fused_computation.31 | loop fusion | flops 22018560 | bytes 20471808 | tf_op jit(solution)/shard_map/reduce_sum | solution.py:439
  115.8 4.5 %shard_map.281 = f32[768,128]{1,0:T(8,128)S(1)} custom-call(f32[1024,768]{1,0:T(8,128)S(1)} %get-tuple-element.115.dy_ref, f32[1024,12]{1,0:T(8,128)S(1)} %get-tuple-element.32.cum_ref, f32[1024,256]{1,0:T(8,128)S(1)} %copy-done.8), custom_call_target="tpu_custom_call" | custom-call | flops 3221225472 | bytes 16777216 | tf_op jit(solution)/shard_map/pallas_call | solution.py:427
  135.8 6.1 %copy.84 = f32[768,1536]{1,0:T(8,128)} copy(f32[768,1536]{0,1:T(8,128)} %pad_maximum_fusion) | data formatting | bytes 9437184
  146.5 22.0 %shard_map.282 = (f32[1024,768]{1,0:T(8,128)}, f32[1024,256]{1,0:T(8,128)S(1)}, f32[1024,12]{1,0:T(8,128)S(1)}, f32[1024,12]{1,0:T(8,128)S(1)}) custom-call(f32[1024,768]{1,0:T(8,128)} %copy-done.2, f32[1024,12]{1,0:T(8,128)S(1)} %copy-done.5, f32[1024,12]{1,0:T(8,128)S(1)} %get-tuple-element.32.cum_ref, f32[12,1024]{1,0:T(8,128)S(1)} %bitcast.44, ...), custom_call_target="tpu_custom_call" | custom-call | flops 12884901888 | bytes 16777216 | tf_op jit(solution)/shard_map/pallas_call | solution.py:443
  171.8 40.1 %collective-permute-done.12 = f32[1024,768]{1,0:T(8,128)} collective-permute-done((f32[1024,768]{1,0:T(8,128)S(1)}, f32[1024,768]{1,0:T(8,128)}, u32[]{:S(2)}, u32[]{:S(2)}) %collective-permute-start.12) | collective-permute-done | bytes 3145760 | tf_op jit(solution)/shard_map/ppermute | solution.py:354
  211.9 4.0 add.246
  222.8 4.9 %collective-permute-done.13 = f32[3,1024]{1,0:T(4,128)S(1)} collective-permute-done((f32[3,1024]{1,0:T(4,128)S(1)}, f32[3,1024]{1,0:T(4,128)S(1)}, u32[]{:S(2)}, u32[]{:S(2)}) %collective-permute-start.13) | collective-permute-done | bytes 12320 | tf_op jit(solution)/shard_map/ppermute | solution.py:25
  232.4 5.8 %fusion.42 = f32[768,1036]{1,0:T(8,128)} fusion(bf16[1024,1036]{1,0:T(8,128)(2,1)} %fusion, bf16[1024,768]{1,0:T(8,128)(2,1)S(1)} %copy-done.18, f32[768]{0:T(1024)S(1)} %copy-done.34, f32[1024]{0:T(1024)S(1)} %get-tuple-element.162), kind=kOutput, calls=%fused_computation.151 | convolution fusion | flops 1632632832 | bytes 6884352 | tf_op jit(solution)/shard_map/dot_general | solution.py:350
  241.6 3.9 convolution_add_fusion
  250.7 11.2 %collective-permute-done.21 = f32[96,1536]{1,0:T(8,128)S(1)} collective-permute-done((f32[96,1536]{1,0:T(8,128)S(1)}, f32[96,1536]{1,0:T(8,128)S(1)}, u32[]{:S(2)}, u32[]{:S(2)}) %collective-permute-start.21) | collective-permute-done | bytes 589856 | tf_op jit(solution)/shard_map/ppermute | solution.py:326
  267.6 45.7 %collective-permute-done.14 = f32[1024,768]{1,0:T(8,128)} collective-permute-done((f32[1024,768]{1,0:T(8,128)}, f32[1024,768]{1,0:T(8,128)}, u32[]{:S(2)}, u32[]{:S(2)}) %collective-permute-start.14) | collective-permute-done | bytes 3145760 | tf_op jit(solution)/shard_map/ppermute | solution.py:354
  313.3 4.2 fusion.13
  321.8 4.4 %collective-permute-start.16 = (f32[11336]{0:T(1024)S(1)}, f32[11336]{0:T(1024)S(1)}, u32[]{:S(2)}, u32[]{:S(2)}) collective-permute-start(f32[11336]{0:T(1024)S(1)} %add.253), channel_id=1, source_target_pairs={{0,4},{2,6},{4,0},{6,2},{1,5},{3,7},{5,1},{7,3},{8,12},{10,14},{12... | collective-permute-start | bytes 136040 | tf_op jit(solution)/shard_map/ppermute | solution.py:314
  344.5 5.6 %fusion.10 = (f32[1024,768]{1,0:T(8,128)}, bf16[1024,768]{1,0:T(8,128)(2,1)}) fusion(bf16[1024,768]{1,0:T(8,128)(2,1)S(1)} %copy-done.18, bf16[1024,768]{1,0:T(8,128)(2,1)} %param.31, f32[1024]{0:T(1024)S(1)} %broadcast_multiply_fusion.9, f32[1024]{0:T(1024)S(1)} %get-tuple-element.161, f32[1024]{0:T(1024)S(1)} %get-tuple-element.162, ...), kind=kLoop, calls=%fused_computation.22 | loop fusion | flops 8650752 | bytes 17316864 | tf_op jit(solution)/shard_map/sub | solution.py:476
  354.7 10.0 %collective-permute-done.23 = f32[48,1536]{1,0:T(8,128)S(1)} collective-permute-done((f32[48,1536]{1,0:T(8,128)S(1)}, f32[48,1536]{1,0:T(8,128)S(1)}, u32[]{:S(2)}, u32[]{:S(2)}) %collective-permute-start.23) | collective-permute-done | bytes 294944 | tf_op jit(solution)/shard_map/ppermute | solution.py:339
  368.3 9.8 %collective-permute-done.26 = f32[48,1036]{1,0:T(8,128)S(1)} collective-permute-done((f32[48,1036]{1,0:T(8,128)S(1)}, f32[48,1036]{1,0:T(8,128)S(1)}, u32[]{:S(2)}, u32[]{:S(2)}) %collective-permute-start.26) | collective-permute-done | bytes 198944 | tf_op jit(solution)/shard_map/ppermute | solution.py:326
  381.8 8.5 %collective-permute-done.27 = f32[48,1036]{1,0:T(8,128)S(1)} collective-permute-done((f32[48,1036]{1,0:T(8,128)S(1)}, f32[48,1036]{1,0:T(8,128)S(1)}, u32[]{:S(2)}, u32[]{:S(2)}) %collective-permute-start.27) | collective-permute-done | bytes 198944 | tf_op jit(solution)/shard_map/ppermute | solution.py:339
  390.5 10.4 %collective-permute-done.24 = f32[96,1536]{1,0:T(8,128)} collective-permute-done((f32[96,1536]{1,0:T(8,128)}, f32[96,1536]{1,0:T(8,128)}, u32[]{:S(2)}, u32[]{:S(2)}) %collective-permute-start.24) | collective-permute-done | bytes 589856 | tf_op jit(solution)/shard_map/ppermute | solution.py:339
  405.1 4.3 %collective-permute-done.28 = f32[96,1036]{1,0:T(8,128)} collective-permute-done((f32[96,1036]{1,0:T(8,128)S(1)}, f32[96,1036]{1,0:T(8,128)}, u32[]{:S(2)}, u32[]{:S(2)}) %collective-permute-start.28) | collective-permute-done | bytes 397856 | tf_op jit(solution)/shard_map/ppermute | solution.py:339
  (268 shorter events, 136.4 us)
Async XLA Ops:
  7.2 26.5 %all-gather.3.cloned.1.call-start = ((), (), s32[]{:S(2)}) async-start(), calls=%async_computation.2 | async-start | bytes 2211840 | tf_op jit(solution)/shard_map/all_gather | solution.py:377
  10.0 80.4 %all-gather.5.cloned.1.call-start = ((), (), s32[]{:S(2)}) async-start(), calls=%async_computation.3 | async-start | bytes 2949120 | tf_op jit(solution)/shard_map/all_gather | solution.py:380
  12.0 217.4 %reduce-scatter.7.cloned.1.call-start = ((), (), s32[]{:S(2)}) async-start(), calls=%async_computation.5 | async-start | bytes 5898240
  51.5 21.7 %collective-permute-start.5 = (f32[768,128]{1,0:T(8,128)S(1)}, f32[768,128]{1,0:T(8,128)S(1)}, u32[]{:S(2)}, u32[]{:S(2)}) collective-permute-start(f32[768,128]{1,0:T(8,128)S(1)} %get-tuple-element.33), channel_id=1, source_target_pairs={{0,6},{1,7},{8,14},{9,15},{16,22},{17,23},{24,30},{25,31}} | collective-permute-start | bytes 1179656 | tf_op jit(solution)/shard_map/ppermute | solution.py:25
  53.0 20.2 %collective-permute-start.3 = (f32[768,128]{1,0:T(8,128)S(1)}, f32[768,128]{1,0:T(8,128)S(1)}, u32[]{:S(2)}, u32[]{:S(2)}) collective-permute-start(f32[768,128]{1,0:T(8,128)S(1)} %get-tuple-element.33), channel_id=1, source_target_pairs={{0,4},{2,6},{1,5},{3,7},{8,12},{10,14},{9,13},{11,15},{16,20},{18,... | collective-permute-start | bytes 1179656 | tf_op jit(solution)/shard_map/ppermute | solution.py:25
  55.9 17.4 %collective-permute-start.1 = (f32[768,128]{1,0:T(8,128)S(1)}, f32[768,128]{1,0:T(8,128)}, u32[]{:S(2)}, u32[]{:S(2)}) collective-permute-start(f32[768,128]{1,0:T(8,128)S(1)} %get-tuple-element.33), channel_id=1, source_target_pairs={{0,2},{2,4},{4,6},{1,3},{3,5},{5,7},{8,10},{10,12},{12,14},{9,11},... | collective-permute-start | bytes 1179656 | tf_op jit(solution)/shard_map/ppermute | solution.py:25
  58.1 14.8 %collective-permute-start.4 = (f32[12]{0:T(128)S(1)}, f32[12]{0:T(128)S(1)}, u32[]{:S(2)}, u32[]{:S(2)}) collective-permute-start(f32[12]{0:T(128)S(1)} %exp.29), channel_id=1, source_target_pairs={{0,4},{2,6},{1,5},{3,7},{8,12},{10,14},{9,13},{11,15},{16,20},{18,... | collective-permute-start | bytes 152 | tf_op jit(solution)/shard_map/ppermute | solution.py:25
  100.7 7.7 %collective-permute-start.6 = (f32[2,1024]{1,0:T(2,128)S(1)}, f32[2,1024]{1,0:T(2,128)S(1)}, u32[]{:S(2)}, u32[]{:S(2)}) collective-permute-start(f32[2,1024]{1,0:T(2,128)S(1)} %pad_maximum_fusion.10), channel_id=1, source_target_pairs={{0,1},{1,0},{2,3},{3,2},{4,5},{5,4},{6,7},{7,6},{8,9},{9,8},{10,11... | collective-permute-start | bytes 24584 | tf_op jit(solution)/shard_map/ppermute | solution.py:354
  120.3 11.4 %collective-permute-start.11 = (f32[768,128]{1,0:T(8,128)S(1)}, f32[768,128]{1,0:T(8,128)S(1)}, u32[]{:S(2)}, u32[]{:S(2)}) collective-permute-start(f32[768,128]{1,0:T(8,128)S(1)} %shard_map.281), channel_id=1, source_target_pairs={{6,0},{7,1},{14,8},{15,9},{22,16},{23,17},{30,24},{31,25}} | collective-permute-start | bytes 1179656 | tf_op jit(solution)/shard_map/ppermute | solution.py:25
  121.6 13.9 %collective-permute-start.9 = (f32[768,128]{1,0:T(8,128)S(1)}, f32[768,128]{1,0:T(8,128)S(1)}, u32[]{:S(2)}, u32[]{:S(2)}) collective-permute-start(f32[768,128]{1,0:T(8,128)S(1)} %shard_map.281), channel_id=1, source_target_pairs={{4,0},{6,2},{5,1},{7,3},{12,8},{14,10},{13,9},{15,11},{20,16},{22,... | collective-permute-start | bytes 1179656 | tf_op jit(solution)/shard_map/ppermute | solution.py:25
  122.9 12.6 %collective-permute-start.7 = (f32[768,128]{1,0:T(8,128)S(1)}, f32[768,128]{1,0:T(8,128)S(1)}, u32[]{:S(2)}, u32[]{:S(2)}) collective-permute-start(f32[768,128]{1,0:T(8,128)S(1)} %shard_map.281), channel_id=1, source_target_pairs={{2,0},{4,2},{6,4},{3,1},{5,3},{7,5},{10,8},{12,10},{14,12},{11,9},... | collective-permute-start | bytes 1179656 | tf_op jit(solution)/shard_map/ppermute | solution.py:25
  142.0 192.0 %reduce-scatter.5.cloned.1.call-start = ((), (), s32[]{:S(2)}) async-start(), calls=%async_computation.4 | async-start | bytes 4423680 | tf_op jit(solution)/shard_map/reduce_scatter | solution.py:464
  146.1 65.8 %collective-permute-start.12 = (f32[1024,768]{1,0:T(8,128)S(1)}, f32[1024,768]{1,0:T(8,128)}, u32[]{:S(2)}, u32[]{:S(2)}) collective-permute-start(f32[1024,768]{1,0:T(8,128)S(1)} %fusion.25), channel_id=1, source_target_pairs={{0,1},{1,0},{2,3},{3,2},{4,5},{5,4},{6,7},{7,6},{8,9},{9,8},{10,11... | collective-permute-start | bytes 9437192 | tf_op jit(solution)/shard_map/ppermute | solution.py:354
  220.0 7.8 %collective-permute-start.13 = (f32[3,1024]{1,0:T(4,128)S(1)}, f32[3,1024]{1,0:T(4,128)S(1)}, u32[]{:S(2)}, u32[]{:S(2)}) collective-permute-start(f32[3,1024]{1,0:T(4,128)S(1)} %add_multiply_fusion.1), channel_id=1, source_target_pairs={{2,0},{4,2},{6,4},{3,1},{5,3},{7,5},{10,8},{12,10},{14,12},{11,9},... | collective-permute-start | bytes 36872 | tf_op jit(solution)/shard_map/ppermute | solution.py:25
  245.5 67.8 %collective-permute-start.14 = (f32[1024,768]{1,0:T(8,128)}, f32[1024,768]{1,0:T(8,128)}, u32[]{:S(2)}, u32[]{:S(2)}) collective-permute-start(f32[1024,768]{1,0:T(8,128)} %convolution_add_fusion), channel_id=1, source_target_pairs={{0,1},{1,0},{2,3},{3,2},{4,5},{5,4},{6,7},{7,6},{8,9},{9,8},{10,11... | collective-permute-start | bytes 9437192 | tf_op jit(solution)/shard_map/ppermute | solution.py:354
  248.6 13.3 %collective-permute-start.21 = (f32[96,1536]{1,0:T(8,128)S(1)}, f32[96,1536]{1,0:T(8,128)S(1)}, u32[]{:S(2)}, u32[]{:S(2)}) collective-permute-start(f32[96,1536]{1,0:T(8,128)S(1)} %copy.69), channel_id=1, source_target_pairs={{0,8},{8,0},{16,24},{24,16},{1,9},{9,1},{17,25},{25,17},{2,10},{10... | collective-permute-start | bytes 1769480 | tf_op jit(solution)/shard_map/ppermute | solution.py:326
  264.7 61.6 %collective-permute-start.22 = (f32[48,1536]{1,0:T(8,128)S(1)}, f32[48,1536]{1,0:T(8,128)}, u32[]{:S(2)}, u32[]{:S(2)}) collective-permute-start(f32[48,1536]{1,0:T(8,128)S(1)} %copy.71), channel_id=1, source_target_pairs={{0,16},{8,24},{16,0},{24,8},{1,17},{9,25},{17,1},{25,9},{2,18},{10... | collective-permute-start | bytes 884744 | tf_op jit(solution)/shard_map/ppermute | solution.py:326
  336.6 13.4 %collective-permute-start.19 = (f32[11336]{0:T(1024)S(1)}, f32[11336]{0:T(1024)S(1)}, u32[]{:S(2)}, u32[]{:S(2)}) collective-permute-start(f32[11336]{0:T(1024)S(1)} %add.256), channel_id=1, source_target_pairs={{0,16},{8,24},{16,0},{24,8},{1,17},{9,25},{17,1},{25,9},{2,18},{10... | collective-permute-start | bytes 136040 | tf_op jit(solution)/shard_map/ppermute | solution.py:314
  343.4 22.5 %collective-permute-start.25 = (f32[96,1036]{1,0:T(8,128)}, f32[96,1036]{1,0:T(8,128)}, u32[]{:S(2)}, u32[]{:S(2)}) collective-permute-start(f32[96,1036]{1,0:T(8,128)} %slice_select_fusion.2), channel_id=1, source_target_pairs={{0,8},{8,0},{16,24},{24,16},{1,9},{9,1},{17,25},{25,17},{2,10},{10... | collective-permute-start | bytes 1193480 | tf_op jit(solution)/shard_map/ppermute | solution.py:326
  352.1 12.6 %collective-permute-start.23 = (f32[48,1536]{1,0:T(8,128)S(1)}, f32[48,1536]{1,0:T(8,128)S(1)}, u32[]{:S(2)}, u32[]{:S(2)}) collective-permute-start(f32[48,1536]{1,0:T(8,128)S(1)} %copy.73), channel_id=1, source_target_pairs={{0,16},{8,24},{16,0},{24,8},{1,17},{9,25},{17,1},{25,9},{2,18},{10... | collective-permute-start | bytes 884744 | tf_op jit(solution)/shard_map/ppermute | solution.py:339
  367.0 11.1 %collective-permute-start.26 = (f32[48,1036]{1,0:T(8,128)S(1)}, f32[48,1036]{1,0:T(8,128)S(1)}, u32[]{:S(2)}, u32[]{:S(2)}) collective-permute-start(f32[48,1036]{1,0:T(8,128)S(1)} %slice_select_fusion.3), channel_id=1, source_target_pairs={{0,16},{8,24},{16,0},{24,8},{1,17},{9,25},{17,1},{25,9},{2,18},{10... | collective-permute-start | bytes 596744 | tf_op jit(solution)/shard_map/ppermute | solution.py:326
  378.2 12.1 %collective-permute-start.27 = (f32[48,1036]{1,0:T(8,128)S(1)}, f32[48,1036]{1,0:T(8,128)S(1)}, u32[]{:S(2)}, u32[]{:S(2)}) collective-permute-start(f32[48,1036]{1,0:T(8,128)S(1)} %select_add_fusion.3), channel_id=1, source_target_pairs={{0,16},{8,24},{16,0},{24,8},{1,17},{9,25},{17,1},{25,9},{2,18},{10... | collective-permute-start | bytes 596744 | tf_op jit(solution)/shard_map/ppermute | solution.py:339
  379.6 21.3 %collective-permute-start.24 = (f32[96,1536]{1,0:T(8,128)}, f32[96,1536]{1,0:T(8,128)}, u32[]{:S(2)}, u32[]{:S(2)}) collective-permute-start(f32[96,1536]{1,0:T(8,128)} %copy.76), channel_id=1, source_target_pairs={{0,8},{8,0},{16,24},{24,16},{1,9},{9,1},{17,25},{25,17},{2,10},{10... | collective-permute-start | bytes 1769480 | tf_op jit(solution)/shard_map/ppermute | solution.py:339
  390.4 19.1 %collective-permute-start.28 = (f32[96,1036]{1,0:T(8,128)S(1)}, f32[96,1036]{1,0:T(8,128)}, u32[]{:S(2)}, u32[]{:S(2)}) collective-permute-start(f32[96,1036]{1,0:T(8,128)S(1)} %pad_maximum_fusion.8), channel_id=1, source_target_pairs={{0,8},{8,0},{16,24},{24,16},{1,9},{9,1},{17,25},{25,17},{2,10},{10... | collective-permute-start | bytes 1193480 | tf_op jit(solution)/shard_map/ppermute | solution.py:339
  (54 other events, 506.2 us)
Sparse Core Ops, SparseCore 0:
  10.2 23.4 all-gather.2
  35.8 24.0 all-gather.4
  142.1 52.8 reduce-scatter.6
  238.3 43.4 reduce-scatter.4

commit v3 on v2

--- a/solution.py
+++ b/solution.py
@@ -350,8 +350,12 @@
     return lax.dot_general(normed, grad_low, TN, preferred_element_type=jnp.float32)
 
 
+def from_col(part):
+    return lax.ppermute(part, "col", [(0, 1), (1, 0)])
+
+
 def col_sum(part):
-    return part + lax.ppermute(part, "col", [(0, 1), (1, 0)])
+    return part + from_col(part)
 
 
 def body(
@@ -429,7 +433,7 @@
     )(grad_y, cumulative, bc_conv)
     mixed_low = (gated * gate_scale * gate_gain).astype(jnp.bfloat16)
     partial_out = right_product(mixed_low, out_full)
-    summed_out = col_sum(partial_out)
+    other_out = from_col(partial_out)
     grad_gate_pre = grad_gated * y_flat * sigmoid_gate * (1.0 + gate_pre * (1.0 - sigmoid_gate))
     gate_low = grad_gate_pre.astype(jnp.bfloat16)
     early_part = jnp.concatenate(
@@ -446,8 +450,6 @@
         ("wide", "bc", "head", "head"),
         backward=True, scratch=(state_shape, (SPAN, SPAN)), flops=16384,
     )(x_conv, step_size, cumulative, cumulative_t, bc_conv, grad_y, y_scan, states, later_grad)
-    grad_x, summed_out = lax.optimization_barrier((grad_x, summed_out))
-    mixed_out = (source + summed_out).astype(jnp.bfloat16)
     (
         grad_value_pre, grad_state_pre, grad_step_pre, grad_rim,
         grad_value_kernel, grad_value_bias, grad_state_kernel, grad_state_bias,
@@ -460,16 +462,18 @@
     scan_low, early = lax.optimization_barrier((scan_low, early))
     early = halves_in(early, "dp")
     grad_normed_part = right_product(gate_low, gate_full) + right_product(scan_low, scan_weights)
-    grad_normed = col_sum(grad_normed_part)
+    grad_normed_part, other_out = lax.optimization_barrier((grad_normed_part, other_out))
+    mixed_out = (source + (partial_out + other_out)).astype(jnp.bfloat16)
+    other_grad = from_col(grad_normed_part)
     late = lax.psum_scatter(
         left_product(normed, scan_low), "row", scatter_dimension=0, tiled=True
-    )
-    late = jnp.concatenate(
-        [late[:, :value_width], col_sum(late[:, value_width:wide]), late[:, wide:]], axis=1
     )
     late, early = lax.optimization_barrier((late, early))
     early = halves_out(early, "dp")
     late = halves_out(halves_in(late, "dp"), "dp")
+    late, other_grad = lax.optimization_barrier((late, other_grad))
+    late_state = col_sum(late[:, value_width:wide])
+    grad_normed = grad_normed_part + other_grad
     gained_in = grad_normed * norm_gain
     input_inner = jnp.sum(gained_in * source, axis=1, keepdims=True)
     input_grad = (
@@ -511,7 +515,7 @@
         norm_gain_grad,
         early[:, value_width:],
         late[:, :value_width],
-        late[:, value_width:wide],
+        late_state,
         late[:, wide:],
         grad_value_kernel,
         grad_value_bias,

time: 426 us -> 399 us (0.937)
  waiting for transfers between devices: 192 us -> 144 us
  local copies, waits for them, and re-layouts: 33.5 us -> 42.5 us
  matrix products: 31.5 us -> 38.2 us
  other arithmetic: 57.9 us -> 64 us
    ppermute x4, waiting for transfers between devices: 85.8 us -> 43.6 us  [from_col(): return lax.ppermute(part, 'col', [(0, 1), (1, 0)])]
    ppermute x4, waiting for transfers between devices: 33.3 us -> 22 us  [halves_out(): given = lax.ppermute(part, axis, [(i, i ^ by) for i in range(peers)])]
    unnamed x96 -> x100, local copies, waits for them, and re-layouts: 16.6 us -> 25.8 us
    ppermute x5, starting transfers between devices: 12.6 us -> 5.3 us  [butterfly(): part = part + lax.ppermute(part, axis, [(i, i ^ by) for i in range(peers)])]
    dot_general x3, matrix products: 11 us -> 17.7 us  [right_product(): lax.dot_general(grad_low, full_weight, NT, preferred_element_type=jnp.flo...]
    unnamed x5, waiting for transfers between devices: 0.07 us -> 5.54 us
  transfers between devices with their start and end apart: 33 -> 33, of which waited for: 20 -> 20; matrix products, arithmetic and copies ran while one was open for 19% -> 23% of each run, Pallas kernels for 10% -> 10%
where the time goes in v3:
time: 399 us; the launch traced here: 392 us
  waiting for transfers between devices  144 us (36%)
  other arithmetic  64 us (16%)
  Pallas kernels  44.5 us (11%)
  starting transfers between devices  43.8 us (11%)
  local copies, waits for them, and re-layouts  42.5 us (11%)
  matrix products  38.2 us (10%)
  between operations  15 us (4%)
    ppermute x4, waiting for transfers between devices, from_col(): return lax.ppermute(part, 'col', [(0, 1), (1, 0)])  43.6 us
    unnamed x100, local copies, waits for them, and re-layouts  25.8 us
    ppermute x12, waiting for transfers between devices, from_behind(): return lax.ppermute(x, axis, pairs)  24 us
    pallas_call x1, Pallas kernels, body(): chunk_call(backward_kernel, head_part, amount, ('wide', 'head', 'head', '...  22.1 us
    ppermute x4, waiting for transfers between devices, halves_out(): given = lax.ppermute(part, axis, [(i, i ^ by) for i in range(peers)])  22 us
    all_gather x1, waiting for transfers between devices, body(): lax.all_gather(jnp.concatenate([value_weight, state_weight, step_weight],...  21.1 us
    ppermute x4, waiting for transfers between devices, halves_in(): lax.ppermute(jnp.where(odd, first, second), axis, [(i, i ^ by) for i in r...  21 us
    ppermute x12, starting transfers between devices, from_behind(): return lax.ppermute(x, axis, pairs)  19.6 us
  transfers between devices with their start and end apart: 33, of which 20 were waited for; matrix products, arithmetic and copies ran while one was open for 23% of the time, Pallas kernels for 10%

profile of v3, /device:TPU:0, one launch (start us, length us, event | category | flops | bytes accessed | tf_op | source)
XLA Modules:
  0.0 392.2 jit_solution(16188880707670888623)
XLA Ops:
  12.6 21.1 %all-gather.3.cloned.1.call-done = bf16[768,1036]{1,0:T(8,128)(2,1)} async-done(((bf16[192,1036]{1,0:T(8,128)(2,1)}), bf16[768,1036]{1,0:T(8,128)(2,1)}) %all-gather.3.cloned.1.call-update) | async-done | bytes 1591312 | tf_op jit(solution)/shard_map/all_gather | solution.py:381
  46.0 5.5 %shard_map.279 = (f32[1024,12]{1,0:T(8,128)S(1)}, f32[768,128]{1,0:T(8,128)S(1)}) custom-call(f32[1024,768]{1,0:T(8,128)S(1)} %get-tuple-element.130.x_ref, f32[1024,12]{1,0:T(8,128)S(1)} %get-tuple-element.127.dt_ref, f32[1024,12]{1,0:T(8,128)S(1)} %get-tuple-element.126.ld_ref, f32[1024,256]{1,0:T(8,128)S(1)} %get-tuple-element.128.bc_ref), custom_call_target="tpu_custom_call" | custom-call | flops 3221225472 | bytes 16777216 | tf_op jit(solution)/shard_map/pallas_call | solution.py:405
  61.6 11.2 %collective-permute-done.4 = f32[12]{0:T(128)S(1)} collective-permute-done((f32[12]{0:T(128)S(1)}, f32[12]{0:T(128)S(1)}, u32[]{:S(2)}, u32[]{:S(2)}) %collective-permute-start.4) | collective-permute-done | bytes 80 | tf_op jit(solution)/shard_map/ppermute | solution.py:25
  76.8 12.4 %shard_map.280 = (f32[1024,768]{1,0:T(8,128)}, f32[4,768,128]{2,1,0:T(8,128)S(1)}) custom-call(f32[1024,768]{1,0:T(8,128)} %copy-done.2, f32[1024,12]{1,0:T(8,128)S(1)} %copy-done.4, f32[1024,12]{1,0:T(8,128)S(1)} %get-tuple-element.34.cum_ref, f32[12,1024]{1,0:T(8,128)S(1)} %bitcast.43, f32[1024,256]{1,0:T(8,128)S(1)} %copy-done.7, ...), custom_call_target="tpu_custom_call" | custom-call | flops 3221225472 | bytes 16777216 | tf_op jit(solution)/shard_map/pallas_call | solution.py:412
  95.8 4.9 %multiply_reduce_fusion.6 = (f32[1024]{0:T(1024)S(1)}, f32[1024]{0:T(1024)S(1)}, f32[1024,768]{1,0:T(8,128)}, f32[768,1024]{0,1:T(8,128)}) fusion(f32[768]{0:T(1024)S(1)} %copy-done.38, f32[1024,768]{1,0:T(8,128)S(1)} %fusion.31, f32[1024,768]{1,0:T(8,128)S(1)} %copy-done.29, f32[1024,768]{1,0:T(8,128)S(1)} %copy-done.14, f32[768]{0:T(1024)S(1)} %mul.475, ...), kind=kOutput, calls=%fused_computation.41 | convolution fusion | flops 1220540416 | bytes 18497536 | tf_op jit(solution)/shard_map/dot_general | solution.py:419
  108.4 7.3 %multiply_reduce_fusion = (f32[768]{0:T(1024)S(1)}, f32[1024,768]{1,0:T(8,128)S(1)}, bf16[1024,768]{1,0:T(8,128)(2,1)S(1)}, f32[768]{0:T(1024)S(1)}) fusion(f32[1024,768]{1,0:T(8,128)} %get-tuple-element.131, f32[1024,768]{1,0:T(8,128)} %copy-done.30, f32[1024]{0:T(1024)S(1)} %bitcast.49, f32[1024,768]{1,0:T(8,128)} %get-tuple-element.124, ...), kind=kLoop, calls=%fused_computation.31 | loop fusion | flops 22018560 | bytes 20471808 | tf_op jit(solution)/shard_map/reduce_sum | solution.py:443
  115.7 4.5 %shard_map.281 = f32[768,128]{1,0:T(8,128)S(1)} custom-call(f32[1024,768]{1,0:T(8,128)S(1)} %get-tuple-element.119.dy_ref, f32[1024,12]{1,0:T(8,128)S(1)} %get-tuple-element.34.cum_ref, f32[1024,256]{1,0:T(8,128)S(1)} %copy-done.8), custom_call_target="tpu_custom_call" | custom-call | flops 3221225472 | bytes 16777216 | tf_op jit(solution)/shard_map/pallas_call | solution.py:431
  135.7 6.1 %copy.84 = f32[768,1536]{1,0:T(8,128)} copy(f32[768,1536]{0,1:T(8,128)} %pad_maximum_fusion) | data formatting | bytes 9437184
  144.7 22.1 %shard_map.282 = (f32[1024,768]{1,0:T(8,128)}, f32[1024,256]{1,0:T(8,128)S(1)}, f32[1024,12]{1,0:T(8,128)S(1)}, f32[1024,12]{1,0:T(8,128)S(1)}) custom-call(f32[1024,768]{1,0:T(8,128)} %copy-done.2, f32[1024,12]{1,0:T(8,128)S(1)} %copy-done.5, f32[1024,12]{1,0:T(8,128)S(1)} %get-tuple-element.34.cum_ref, f32[12,1024]{1,0:T(8,128)S(1)} %bitcast.44, ...), custom_call_target="tpu_custom_call" | custom-call | flops 12884901888 | bytes 16777216 | tf_op jit(solution)/shard_map/pallas_call | solution.py:447
  173.5 4.5 %multiply_reduce_fusion.3 = (f32[768]{0:T(1024)S(1)}, f32[768]{0:T(1024)S(1)}, f32[768]{0:T(1024)S(1)}, f32[768]{0:T(1024)S(1)}, f32[768]{0:T(1024)S(1)}, /*index=5*/f32[1024,768]{1,0:T(8,128)S(1)}) fusion(f32[1024,768]{1,0:T(8,128)S(1)} %copy-done.13, f32[3,768]{1,0:T(4,128)S(1)} %slice.189, f32[1024,1036]{1,0:T(8,128)} %copy-done.16, ...), kind=kLoop, calls=%fused_computation.34 | loop fusion | flops 18084096 | bytes 18902016 | tf_op jit(solution)/shard_map/transpose(jvp())/reduce_sum | solution.py:55
  189.6 5.5 %reduce-scatter.7.cloned.1.call-done = f32[192,1536]{1,0:T(8,128)} async-done(((f32[768,1536]{1,0:T(8,128)}), f32[192,1536]{1,0:T(8,128)}) %reduce-scatter.7.cloned.1.call-update) | async-done | bytes 1179664
  198.0 5.8 %fusion.40 = f32[768,1036]{1,0:T(8,128)} fusion(bf16[1024,1036]{1,0:T(8,128)(2,1)} %fusion, bf16[1024,768]{1,0:T(8,128)(2,1)S(1)} %copy-done.18, f32[768]{0:T(1024)S(1)} %copy-done.39, f32[1024]{0:T(1024)S(1)} %get-tuple-element.166), kind=kOutput, calls=%fused_computation.144 | convolution fusion | flops 1632632832 | bytes 6884352 | tf_op jit(solution)/shard_map/dot_general | solution.py:350
  207.5 5.9 %fusion.25 = f32[1024,768]{1,0:T(8,128)} fusion(bf16[768,1536]{1,0:T(8,128)(2,1)} %all-gather.5.cloned.1.call-done, f32[1024,768]{1,0:T(8,128)} %get-tuple-element.124, f32[1024]{0:T(1024)S(1)} %bitcast.48, f32[768]{0:T(1024)S(1)} %copy-done.38), kind=kOutput, calls=%fused_computation.77 | convolution fusion | flops 1210318848 | bytes 7478272 | tf_op jit(solution)/shard_map/dot_general | solution.py:346
  214.6 6.6 %collective-permute-done.14 = f32[96,1536]{1,0:T(8,128)S(1)} collective-permute-done((f32[96,1536]{1,0:T(8,128)S(1)}, f32[96,1536]{1,0:T(8,128)S(1)}, u32[]{:S(2)}, u32[]{:S(2)}) %collective-permute-start.14) | collective-permute-done | bytes 589856 | tf_op jit(solution)/shard_map/ppermute | solution.py:326
  226.8 4.8 %fusion.29 = f32[1024,768]{1,0:T(8,128)} fusion(bf16[1024,768]{1,0:T(8,128)(2,1)} %copy-done.35, bf16[768,1536]{1,0:T(8,128)(2,1)} %all-gather.5.cloned.1.call-done), kind=kOutput, calls=%fused_computation.81 | convolution fusion | flops 1207959552 | bytes 5898240 | tf_op jit(solution)/shard_map/dot_general | solution.py:346
  231.9 7.2 %collective-permute-done.15 = f32[48,1536]{1,0:T(8,128)S(1)} collective-permute-done((f32[48,1536]{1,0:T(8,128)S(1)}, f32[48,1536]{1,0:T(8,128)S(1)}, u32[]{:S(2)}, u32[]{:S(2)}) %collective-permute-start.15) | collective-permute-done | bytes 294944 | tf_op jit(solution)/shard_map/ppermute | solution.py:326
  249.8 7.0 %convolution_add_fusion = f32[1024,768]{1,0:T(8,128)} fusion(f32[1024,768]{1,0:T(8,128)} %fusion.29, bf16[1024,1036]{1,0:T(8,128)(2,1)} %fusion, bf16[768,1036]{1,0:T(8,128)(2,1)} %all-gather.3.cloned.1.call-done), kind=kOutput, calls=%fused_computation.48 | convolution fusion | flops 1630273536 | bytes 10004480 | tf_op jit(solution)/shard_map/dot_general | solution.py:346
  256.9 26.0 %collective-permute-done.13 = f32[1024,768]{1,0:T(8,128)} collective-permute-done((f32[1024,768]{1,0:T(8,128)}, f32[1024,768]{1,0:T(8,128)}, u32[]{:S(2)}, u32[]{:S(2)}) %collective-permute-start.13) | collective-permute-done | bytes 3145760 | tf_op jit(solution)/shard_map/ppermute | solution.py:354
  290.7 7.2 %collective-permute-done.17 = f32[48,1036]{1,0:T(8,128)S(1)} collective-permute-done((f32[48,1036]{1,0:T(8,128)S(1)}, f32[48,1036]{1,0:T(8,128)S(1)}, u32[]{:S(2)}, u32[]{:S(2)}) %collective-permute-start.17) | collective-permute-done | bytes 198944 | tf_op jit(solution)/shard_map/ppermute | solution.py:326
  304.8 5.6 %collective-permute-done.18 = f32[48,1036]{1,0:T(8,128)} collective-permute-done((f32[48,1036]{1,0:T(8,128)S(1)}, f32[48,1036]{1,0:T(8,128)}, u32[]{:S(2)}, u32[]{:S(2)}) %collective-permute-start.18) | collective-permute-done | bytes 198944 | tf_op jit(solution)/shard_map/ppermute | solution.py:339
  313.1 10.0 %collective-permute-done.27 = f32[96,1536]{1,0:T(8,128)} collective-permute-done((f32[96,1536]{1,0:T(8,128)}, f32[96,1536]{1,0:T(8,128)}, u32[]{:S(2)}, u32[]{:S(2)}) %collective-permute-start.27) | collective-permute-done | bytes 589856 | tf_op jit(solution)/shard_map/ppermute | solution.py:339
  325.3 6.3 %collective-permute-done.19 = f32[96,1036]{1,0:T(8,128)} collective-permute-done((f32[96,1036]{1,0:T(8,128)}, f32[96,1036]{1,0:T(8,128)}, u32[]{:S(2)}, u32[]{:S(2)}) %collective-permute-start.19) | collective-permute-done | bytes 397856 | tf_op jit(solution)/shard_map/ppermute | solution.py:339
  333.8 17.6 %collective-permute-done.20 = f32[1024,768]{1,0:T(8,128)} collective-permute-done((f32[1024,768]{1,0:T(8,128)}, f32[1024,768]{1,0:T(8,128)}, u32[]{:S(2)}, u32[]{:S(2)}) %collective-permute-start.20) | collective-permute-done | bytes 3145760 | tf_op jit(solution)/shard_map/ppermute | solution.py:354
  367.6 8.1 %fusion.10 = (f32[1024,768]{1,0:T(8,128)}, bf16[1024,768]{1,0:T(8,128)(2,1)}) fusion(bf16[1024,768]{1,0:T(8,128)(2,1)S(1)} %copy-done.18, bf16[1024,768]{1,0:T(8,128)(2,1)} %param.31, f32[1024]{0:T(1024)S(1)} %broadcast_multiply_fusion.9, f32[1024]{0:T(1024)S(1)} %get-tuple-element.165, f32[1024]{0:T(1024)S(1)} %get-tuple-element.166, ...), kind=kLoop, calls=%fused_computation.22 | loop fusion | flops 9437184 | bytes 20462592 | tf_op jit(solution)/shard_map/sub | solution.py:480
  (268 shorter events, 154.0 us)
Async XLA Ops:
  7.2 26.5 %all-gather.3.cloned.1.call-start = ((), (), s32[]{:S(2)}) async-start(), calls=%async_computation.2 | async-start | bytes 2211840 | tf_op jit(solution)/shard_map/all_gather | solution.py:381
  10.0 80.3 %all-gather.5.cloned.1.call-start = ((), (), s32[]{:S(2)}) async-start(), calls=%async_computation.3 | async-start | bytes 2949120 | tf_op jit(solution)/shard_map/all_gather | solution.py:384
  12.0 183.1 %reduce-scatter.7.cloned.1.call-start = ((), (), s32[]{:S(2)}) async-start(), calls=%async_computation.5 | async-start | bytes 5898240
  51.6 21.7 %collective-permute-start.5 = (f32[768,128]{1,0:T(8,128)S(1)}, f32[768,128]{1,0:T(8,128)S(1)}, u32[]{:S(2)}, u32[]{:S(2)}) collective-permute-start(f32[768,128]{1,0:T(8,128)S(1)} %get-tuple-element.35), channel_id=1, source_target_pairs={{0,6},{1,7},{8,14},{9,15},{16,22},{17,23},{24,30},{25,31}} | collective-permute-start | bytes 1179656 | tf_op jit(solution)/shard_map/ppermute | solution.py:25
  53.1 20.2 %collective-permute-start.3 = (f32[768,128]{1,0:T(8,128)S(1)}, f32[768,128]{1,0:T(8,128)S(1)}, u32[]{:S(2)}, u32[]{:S(2)}) collective-permute-start(f32[768,128]{1,0:T(8,128)S(1)} %get-tuple-element.35), channel_id=1, source_target_pairs={{0,4},{2,6},{1,5},{3,7},{8,12},{10,14},{9,13},{11,15},{16,20},{18,... | collective-permute-start | bytes 1179656 | tf_op jit(solution)/shard_map/ppermute | solution.py:25
  55.9 17.3 %collective-permute-start.1 = (f32[768,128]{1,0:T(8,128)S(1)}, f32[768,128]{1,0:T(8,128)}, u32[]{:S(2)}, u32[]{:S(2)}) collective-permute-start(f32[768,128]{1,0:T(8,128)S(1)} %get-tuple-element.35), channel_id=1, source_target_pairs={{0,2},{2,4},{4,6},{1,3},{3,5},{5,7},{8,10},{10,12},{12,14},{9,11},... | collective-permute-start | bytes 1179656 | tf_op jit(solution)/shard_map/ppermute | solution.py:25
  58.1 14.8 %collective-permute-start.4 = (f32[12]{0:T(128)S(1)}, f32[12]{0:T(128)S(1)}, u32[]{:S(2)}, u32[]{:S(2)}) collective-permute-start(f32[12]{0:T(128)S(1)} %exp.29), channel_id=1, source_target_pairs={{0,4},{2,6},{1,5},{3,7},{8,12},{10,14},{9,13},{11,15},{16,20},{18,... | collective-permute-start | bytes 152 | tf_op jit(solution)/shard_map/ppermute | solution.py:25
  120.2 11.4 %collective-permute-start.11 = (f32[768,128]{1,0:T(8,128)S(1)}, f32[768,128]{1,0:T(8,128)S(1)}, u32[]{:S(2)}, u32[]{:S(2)}) collective-permute-start(f32[768,128]{1,0:T(8,128)S(1)} %shard_map.281), channel_id=1, source_target_pairs={{6,0},{7,1},{14,8},{15,9},{22,16},{23,17},{30,24},{31,25}} | collective-permute-start | bytes 1179656 | tf_op jit(solution)/shard_map/ppermute | solution.py:25
  121.5 13.9 %collective-permute-start.9 = (f32[768,128]{1,0:T(8,128)S(1)}, f32[768,128]{1,0:T(8,128)S(1)}, u32[]{:S(2)}, u32[]{:S(2)}) collective-permute-start(f32[768,128]{1,0:T(8,128)S(1)} %shard_map.281), channel_id=1, source_target_pairs={{4,0},{6,2},{5,1},{7,3},{12,8},{14,10},{13,9},{15,11},{20,16},{22,... | collective-permute-start | bytes 1179656 | tf_op jit(solution)/shard_map/ppermute | solution.py:25
  122.8 12.6 %collective-permute-start.7 = (f32[768,128]{1,0:T(8,128)S(1)}, f32[768,128]{1,0:T(8,128)S(1)}, u32[]{:S(2)}, u32[]{:S(2)}) collective-permute-start(f32[768,128]{1,0:T(8,128)S(1)} %shard_map.281), channel_id=1, source_target_pairs={{2,0},{4,2},{6,4},{3,1},{5,3},{7,5},{10,8},{12,10},{14,12},{11,9},... | collective-permute-start | bytes 1179656 | tf_op jit(solution)/shard_map/ppermute | solution.py:25
  141.9 102.5 %reduce-scatter.5.cloned.1.call-start = ((), (), s32[]{:S(2)}) async-start(), calls=%async_computation.4 | async-start | bytes 4423680 | tf_op jit(solution)/shard_map/reduce_scatter | solution.py:468
  179.0 9.0 %collective-permute-start.12 = (f32[3,1024]{1,0:T(4,128)S(1)}, f32[3,1024]{1,0:T(4,128)S(1)}, u32[]{:S(2)}, u32[]{:S(2)}) collective-permute-start(f32[3,1024]{1,0:T(4,128)S(1)} %add_multiply_fusion.1), channel_id=1, source_target_pairs={{2,0},{4,2},{6,4},{3,1},{5,3},{7,5},{10,8},{12,10},{14,12},{11,9},... | collective-permute-start | bytes 36872 | tf_op jit(solution)/shard_map/ppermute | solution.py:25
  206.0 15.1 %collective-permute-start.14 = (f32[96,1536]{1,0:T(8,128)S(1)}, f32[96,1536]{1,0:T(8,128)S(1)}, u32[]{:S(2)}, u32[]{:S(2)}) collective-permute-start(f32[96,1536]{1,0:T(8,128)S(1)} %copy.69), channel_id=1, source_target_pairs={{0,8},{8,0},{16,24},{24,16},{1,9},{9,1},{17,25},{25,17},{2,10},{10... | collective-permute-start | bytes 1769480 | tf_op jit(solution)/shard_map/ppermute | solution.py:326
  213.4 69.4 %collective-permute-start.13 = (f32[1024,768]{1,0:T(8,128)}, f32[1024,768]{1,0:T(8,128)}, u32[]{:S(2)}, u32[]{:S(2)}) collective-permute-start(f32[1024,768]{1,0:T(8,128)} %fusion.25), channel_id=1, source_target_pairs={{0,1},{1,0},{2,3},{3,2},{4,5},{5,4},{6,7},{7,6},{8,9},{9,8},{10,11... | collective-permute-start | bytes 9437192 | tf_op jit(solution)/shard_map/ppermute | solution.py:354
  224.2 14.9 %collective-permute-start.15 = (f32[48,1536]{1,0:T(8,128)S(1)}, f32[48,1536]{1,0:T(8,128)S(1)}, u32[]{:S(2)}, u32[]{:S(2)}) collective-permute-start(f32[48,1536]{1,0:T(8,128)S(1)} %copy.71), channel_id=1, source_target_pairs={{0,16},{8,24},{16,0},{24,8},{1,17},{9,25},{17,1},{25,9},{2,18},{10... | collective-permute-start | bytes 884744 | tf_op jit(solution)/shard_map/ppermute | solution.py:326
  244.6 39.6 %collective-permute-start.26 = (f32[48,1536]{1,0:T(8,128)S(1)}, f32[48,1536]{1,0:T(8,128)S(1)}, u32[]{:S(2)}, u32[]{:S(2)}) collective-permute-start(f32[48,1536]{1,0:T(8,128)S(1)} %copy.73), channel_id=1, source_target_pairs={{0,16},{8,24},{16,0},{24,8},{1,17},{9,25},{17,1},{25,9},{2,18},{10... | collective-permute-start | bytes 884744 | tf_op jit(solution)/shard_map/ppermute | solution.py:339
  248.3 37.1 %collective-permute-start.16 = (f32[96,1036]{1,0:T(8,128)S(1)}, f32[96,1036]{1,0:T(8,128)}, u32[]{:S(2)}, u32[]{:S(2)}) collective-permute-start(f32[96,1036]{1,0:T(8,128)S(1)} %slice_select_fusion.2), channel_id=1, source_target_pairs={{0,8},{8,0},{16,24},{24,16},{1,9},{9,1},{17,25},{25,17},{2,10},{10... | collective-permute-start | bytes 1193480 | tf_op jit(solution)/shard_map/ppermute | solution.py:326
  282.9 68.5 %collective-permute-start.20 = (f32[1024,768]{1,0:T(8,128)}, f32[1024,768]{1,0:T(8,128)}, u32[]{:S(2)}, u32[]{:S(2)}) collective-permute-start(f32[1024,768]{1,0:T(8,128)} %convolution_add_fusion), channel_id=1, source_target_pairs={{0,1},{1,0},{2,3},{3,2},{4,5},{5,4},{6,7},{7,6},{8,9},{9,8},{10,11... | collective-permute-start | bytes 9437192 | tf_op jit(solution)/shard_map/ppermute | solution.py:354
  286.8 11.2 %collective-permute-start.17 = (f32[48,1036]{1,0:T(8,128)S(1)}, f32[48,1036]{1,0:T(8,128)S(1)}, u32[]{:S(2)}, u32[]{:S(2)}) collective-permute-start(f32[48,1036]{1,0:T(8,128)S(1)} %slice_select_fusion.3), channel_id=1, source_target_pairs={{0,16},{8,24},{16,0},{24,8},{1,17},{9,25},{17,1},{25,9},{2,18},{10... | collective-permute-start | bytes 596744 | tf_op jit(solution)/shard_map/ppermute | solution.py:326
  298.0 12.4 %collective-permute-start.18 = (f32[48,1036]{1,0:T(8,128)S(1)}, f32[48,1036]{1,0:T(8,128)}, u32[]{:S(2)}, u32[]{:S(2)}) collective-permute-start(f32[48,1036]{1,0:T(8,128)S(1)} %select_add_fusion.3), channel_id=1, source_target_pairs={{0,16},{8,24},{16,0},{24,8},{1,17},{9,25},{17,1},{25,9},{2,18},{10... | collective-permute-start | bytes 596744 | tf_op jit(solution)/shard_map/ppermute | solution.py:339
  301.7 21.4 %collective-permute-start.27 = (f32[96,1536]{1,0:T(8,128)}, f32[96,1536]{1,0:T(8,128)}, u32[]{:S(2)}, u32[]{:S(2)}) collective-permute-start(f32[96,1536]{1,0:T(8,128)} %copy.76), channel_id=1, source_target_pairs={{0,8},{8,0},{16,24},{24,16},{1,9},{9,1},{17,25},{25,17},{2,10},{10... | collective-permute-start | bytes 1769480 | tf_op jit(solution)/shard_map/ppermute | solution.py:339
  313.0 18.7 %collective-permute-start.19 = (f32[96,1036]{1,0:T(8,128)}, f32[96,1036]{1,0:T(8,128)}, u32[]{:S(2)}, u32[]{:S(2)}) collective-permute-start(f32[96,1036]{1,0:T(8,128)} %pad_maximum_fusion.8), channel_id=1, source_target_pairs={{0,8},{8,0},{16,24},{24,16},{1,9},{9,1},{17,25},{25,17},{2,10},{10... | collective-permute-start | bytes 1193480 | tf_op jit(solution)/shard_map/ppermute | solution.py:339
  364.1 15.3 %collective-permute-start.28 = (f32[192,256]{1,0:T(8,128)S(1)}, f32[192,256]{1,0:T(8,128)S(1)}, u32[]{:S(2)}, u32[]{:S(2)}) collective-permute-start(f32[192,256]{1,0:T(8,128)S(1)} %slice.177), channel_id=1, source_target_pairs={{0,1},{1,0},{2,3},{3,2},{4,5},{5,4},{6,7},{7,6},{8,9},{9,8},{10,11... | collective-permute-start | bytes 589832 | tf_op jit(solution)/shard_map/ppermute | solution.py:354
  366.9 10.4 %collective-permute-start.24 = (f32[11336]{0:T(1024)S(1)}, f32[11336]{0:T(1024)S(1)}, u32[]{:S(2)}, u32[]{:S(2)}) collective-permute-start(f32[11336]{0:T(1024)S(1)} %add.261), channel_id=1, source_target_pairs={{0,8},{8,0},{16,24},{24,16},{1,9},{9,1},{17,25},{25,17},{2,10},{10... | collective-permute-start | bytes 136040 | tf_op jit(solution)/shard_map/ppermute | solution.py:314
  (57 other events, 315.3 us)
Sparse Core Ops, SparseCore 0:
  10.2 23.4 all-gather.2
  35.8 24.0 all-gather.4
  142.0 53.0 reduce-scatter.6
  203.9 40.4 reduce-scatter.4
